TPU v7x, 512 devices: a whole 4x4x16 slice. The times are simulated.
512 devices in a mesh: dom: 128 (over z, y, core), feat: 4 (over x).
Axes of the slice: x: 4, y: 4, z: 16, core: 2. Of those that a mesh axis runs over, the one named last changes fastest.
Arguments:
- features: bfloat16 [65536, 768], P('dom', 'feat'), may hold values from -6 to 6
- w_self: bfloat16 [768, 1024], P(None, 'feat'), may hold values from -0.21875 to 0.21875
- w_neigh: bfloat16 [768, 1024], P(None, 'feat'), may hold values from -0.21875 to 0.21875
- out_bias: float32 [1024], P('feat'), may hold values from -3 to 3
- degrees: int32 [65536], P('dom'), may hold values from 1 to 16
- tile_index: int32 [128, 12, 2], P('dom'), may hold values from 0 to 3
- tile_mask: int32 [128, 12, 128, 128], P('dom'), may hold values 0 or 1
- cut_source: int32 [128, 128, 24], P('dom'), may hold values from 0 to 511
- cut_target: int32 [128, 128, 24], P('dom'), may hold values from -1 to 511, as said below
- hub_local: int32 [128, 4], P('dom'), may hold values from 0 to 511, as said below
- hub_source: int32 [128, 512], P('dom'), may hold values from 0 to 511
- hub_target: int32 [128, 512], P('dom'), may hold values from 0 to 511
- mirror_source: int32 [128, 512], P('dom'), may hold values from 0 to 511
- mirror_target: int32 [128, 512], P('dom'), may hold values from 0 to 511, as said below
Outputs:
- hidden: bfloat16 [65536, 1024], P('dom', 'feat')
Inputs may be any that keep to these rules, and one draw needn't show every extreme that they name: `hub_local`: within each partition the 4 rows are distinct. `cut_target`: slots holding -1 come after the live ones of each pair; for every receiving partition some sending partition fills all 24 slots. `mirror_target`: of one partition's edges, at most 8 go into hubs of any one master partition, and for every partition some master receives exactly 8 of them.
All inputs are finite; a program needn't handle non-finite values. No bound on the sum of `tile_mask` on one device may be relied on, other than what follows from the above.
Results may differ from a plain program's by a relative error of at most 0.0044.
Values may be sent and summed in bfloat16 or wider, within the bound.
A program may use at most 64 MiB of HBM per device.

v0:
```python
import jax
import jax.numpy as jnp
from jax import lax
from jax.sharding import PartitionSpec as P


def on_device(
    features,
    w_self,
    w_neigh,
    out_bias,
    degrees,
    tile_index,
    tile_mask,
    cut_source,
    cut_target,
    hub_local,
    hub_source,
    hub_target,
    mirror_source,
    mirror_target,
):
    nodes_here = features.shape[0]
    columns = features.shape[1]
    tile_len = tile_mask.shape[2]
    block_count = nodes_here // tile_len
    hub_count = hub_local.shape[1]
    node_ids = jnp.arange(nodes_here, dtype=jnp.int32)
    blocks = features.reshape(block_count, tile_len, columns)
    picked = jnp.take(blocks, tile_index[0, :, 1], axis=0)
    products = jnp.einsum(
        "tuv,tvc->tuc",
        tile_mask[0].astype(jnp.bfloat16),
        picked,
        preferred_element_type=jnp.float32,
    )
    owners = (
        jnp.arange(block_count, dtype=jnp.int32)[:, None] == tile_index[0, :, 0][None, :]
    ).astype(jnp.float32)
    local_sum = jnp.dot(
        owners,
        products.reshape(products.shape[0], tile_len * columns),
        precision=lax.Precision.HIGHEST,
    ).reshape(nodes_here, columns)
    outgoing = jnp.take(features, cut_source[0], axis=0)
    targets = cut_target[0].reshape(-1)
    cut_onehot = (node_ids[:, None] == targets[None, :]).astype(jnp.bfloat16)
    arrived = lax.all_to_all(outgoing, "dom", split_axis=0, concat_axis=0, tiled=True)
    flat = arrived.reshape(-1, arrived.shape[2])
    cut_sum = jnp.dot(cut_onehot, flat, preferred_element_type=jnp.float32)
    own_hubs = jnp.take(features, hub_local[0], axis=0)
    hub_table = lax.all_gather(own_hubs, "dom", axis=0, tiled=True)
    hub_vals = jnp.take(hub_table, hub_source[0], axis=0)
    hub_onehot = (node_ids[:, None] == hub_target[0][None, :]).astype(jnp.bfloat16)
    hub_sum = jnp.dot(hub_onehot, hub_vals, preferred_element_type=jnp.float32)
    mirror_vals = jnp.take(features, mirror_source[0], axis=0)
    hub_ids = jnp.arange(hub_table.shape[0], dtype=jnp.int32)
    mirror_onehot = (hub_ids[:, None] == mirror_target[0][None, :]).astype(jnp.bfloat16)
    partial_hubs = jnp.dot(mirror_onehot, mirror_vals, preferred_element_type=jnp.float32)
    summed = lax.psum(partial_hubs, "dom")
    mirrored = lax.dynamic_slice_in_dim(summed, lax.axis_index("dom") * hub_count, hub_count, 0)
    place_hubs = (node_ids[:, None] == hub_local[0][None, :]).astype(jnp.float32)
    master = jnp.dot(place_hubs, mirrored, precision=lax.Precision.HIGHEST)
    mean_rows = (
        (local_sum + cut_sum + hub_sum + master) / degrees.astype(jnp.float32)[:, None]
    ).astype(jnp.bfloat16)
    carry = jnp.dot(
        lax.all_gather(features, "feat", axis=1, tiled=True),
        w_self,
        preferred_element_type=jnp.float32,
    )
    total = carry + jnp.dot(
        lax.all_gather(mean_rows, "feat", axis=1, tiled=True),
        w_neigh,
        preferred_element_type=jnp.float32,
    )
    return jax.nn.relu(total + out_bias[None, :]).astype(jnp.bfloat16)


def solution(mesh):
    return jax.shard_map(
        on_device,
        mesh=mesh,
        in_specs=(
            P("dom", "feat"),
            P(None, "feat"),
            P(None, "feat"),
            P("feat"),
            P("dom"),
            P("dom", None, None),
            P("dom", None, None, None),
            P("dom", None, None),
            P("dom", None, None),
            P("dom", None),
            P("dom", None),
            P("dom", None),
            P("dom", None),
            P("dom", None),
        ),
        out_specs=P("dom", "feat"),
        check_vma=False,
    )
```

profile of v0, /device:TPU:6, one launch (start us, length us, event | category | flops | bytes accessed | tf_op | source)
XLA Modules:
  0.0 416.1 jit_solution(2797662366267209832)
XLA Ops:
  6.5 0.0 copy-start
  6.5 0.8 compare_select_fusion
  7.3 0.7 compare_and_fusion
  8.0 1.1 copy.40
  9.1 0.1 copy.39
  9.2 0.1 reshape.154
  9.3 0.1 copy.38
  9.4 11.1 %gather_fusion.1 = bf16[3072,192]{1,0:T(8,128)(2,1)S(1)} fusion(bf16[512,192]{1,0:T(8,128)(2,1)S(1)} %copy.40, s32[3072]{0:T(1024)S(1)} %broadcast_clamp_fusion), kind=kCustom, calls=%fused_computation.3 | custom fusion | bytes 2371584 | tf_op jit(solution)/shard_map/jit(_take)/gather | solution.py:45
  20.5 1.5 broadcast_select_fusion
  21.9 20.6 %all-to-all-start = ((bf16[128,24,192]{2,1,0:T(8,128)(2,1)}), bf16[128,24,192]{2,1,0:T(8,128)(2,1)}, u32[]{:S(2)}, u32[]{:S(2)}) async-start(bf16[128,24,192]{2,1,0:T(8,128)(2,1)} %broadcast_select_fusion), calls=%async_computation | async-start | bytes 3145728 | tf_op jit(solution)/shard_map/all_to_all | solution.py:48
  42.5 0.0 copy-start.8
  42.5 0.0 all-reduce.2.cloned.1.call-start
  42.6 0.0 copy-start.12
  42.6 2.0 gather_fusion.4
  44.6 0.0 copy-start.10
  44.6 0.0 copy-start.1
  44.6 1.3 fusion.10
  45.9 0.0 all-reduce.2.cloned.1.call-update
  45.9 0.0 copy-done.12
  45.9 0.6 gather_fusion.2
  46.5 0.1 select_bitcast_fusion
  46.6 159.9 %all-gather = bf16[128,4,192]{2,1,0:T(4,128)(2,1)S(1)} all-gather(bf16[1,4,192]{2,1,0:T(4,128)(2,1)S(1)} %select_bitcast_fusion), channel_id=1, replica_groups=mesh['dom'=128,'feat'=4] {'dom'}, dimensions={0}, use_global_device_ids=true | all-gather | bytes 198144 | tf_op jit(solution)/shard_map/all_gather | solution.py:52
  206.5 0.2 reshape.172
  206.7 0.7 gather_fusion
  207.4 0.4 convolution_bitcast_fusion
  207.8 1.6 copy.36
  209.5 2.1 reshape.125
  211.6 0.0 copy-start.3
  211.6 0.0 copy-start.6
  211.6 0.0 copy-start.5
  211.6 0.6 fusion.26
  212.2 0.3 reshape.126
  212.5 0.0 copy-start.9
  212.5 0.2 copy.41
  212.7 0.1 copy.37
  212.8 0.1 eq.78
  213.0 2.0 gather_fusion.3
  215.0 0.5 fusion.9
  215.5 14.5 %all_gather.9 = bf16[512,768]{0,1:T(8,128)(2,1)S(1)} all-gather(bf16[512,192]{0,1:T(8,128)(2,1)S(1)} %copy-done.1), channel_id=1, replica_groups=mesh['dom'=128,'feat'=4] {'feat'}, dimensions={1}, use_global_device_ids=true | all-gather | bytes 983040 | tf_op jit(solution)/shard_map/all_gather | solution.py:68
  230.0 0.4 fusion.34
  230.4 0.0 all-to-all-done
  230.4 2.9 fusion.7
  233.4 0.0 copy-start.7
  233.4 0.0 copy-start.11
  233.4 159.6 %all-reduce.2.cloned.1.call-done = f32[512,192]{1,0:T(8,128)} async-done(((f32[512,192]{1,0:T(8,128)}), f32[512,192]{1,0:T(8,128)}) %all-reduce.2.cloned.1.call-update) | async-done | bytes 393232 | tf_op jit(solution)/shard_map/psum | solution.py:60
  393.0 1.1 fusion.8
  394.1 14.1 %all_gather.11 = bf16[512,768]{0,1:T(8,128)(2,1)S(1)} all-gather(bf16[512,192]{0,1:T(8,128)(2,1)S(1)} %fusion.8), channel_id=1, replica_groups=mesh['dom'=128,'feat'=4] {'feat'}, dimensions={1}, use_global_device_ids=true | all-gather | bytes 983040 | tf_op jit(solution)/shard_map/all_gather | solution.py:73
  408.1 1.1 fusion.4
  (30 shorter events, 0.1 us)
Async XLA Ops:
  6.5 223.4 %copy-start = (bf16[768,256]{1,0:T(8,128)(2,1)S(1)}, bf16[768,256]{1,0:T(8,128)(2,1)}, u32[]{:S(2)}) copy-start(bf16[768,256]{1,0:T(8,128)(2,1)} %param.17) | copy-start | bytes 1179652
  21.9 20.6 %copy-start.4 = (s32[1,512]{1,0:T(1,128)S(1)}, s32[1,512]{1,0:T(1,128)}, u32[]{:S(2)}) copy-start(s32[1,512]{1,0:T(1,128)} %param.28) | copy-start | bytes 6148
  21.9 208.4 %all-to-all-start = ((bf16[128,24,192]{2,1,0:T(8,128)(2,1)}), bf16[128,24,192]{2,1,0:T(8,128)(2,1)}, u32[]{:S(2)}, u32[]{:S(2)}) async-start(bf16[128,24,192]{2,1,0:T(8,128)(2,1)} %broadcast_select_fusion), calls=%async_computation | async-start | bytes 3145728 | tf_op jit(solution)/shard_map/all_to_all | solution.py:48
  42.5 2.1 copy-start.8
  42.5 350.5 %all-reduce.2.cloned.1.call-start = ((), (), s32[]{:S(2)}) async-start(), calls=%async_computation.1 | async-start | bytes 1048576 | tf_op jit(solution)/shard_map/psum | solution.py:60
  42.6 3.3 copy-start.12
  44.6 162.1 %copy-start.10 = (s32[1,12,2]{1,2,0:T(2,128)S(1)}, s32[1,12,2]{1,2,0:T(2,128)}, u32[]{:S(2)}) copy-start(s32[1,12,2]{1,2,0:T(2,128)} %param.21) | copy-start | bytes 292
  44.6 162.1 %copy-start.1 = (bf16[512,192]{0,1:T(8,128)(2,1)S(1)}, bf16[512,192]{0,1:T(8,128)(2,1)}, u32[]{:S(2)}) copy-start(bf16[512,192]{0,1:T(8,128)(2,1)} %param.16) | copy-start | bytes 589828
  45.9 161.5 %copy-start.2 = (s32[1,12,128,128]{3,2,1,0:T(8,128)S(1)}, s32[1,12,128,128]{3,2,1,0:T(8,128)}, u32[]{:S(2)}) copy-start(s32[1,12,128,128]{3,2,1,0:T(8,128)} %param.22) | copy-start | bytes 2359300
  211.6 1.2 copy-start.3
  211.6 1.4 copy-start.6
  211.6 1.4 copy-start.5
  212.5 2.4 copy-start.9
  233.4 174.8 %copy-start.7 = (bf16[768,256]{1,0:T(8,128)(2,1)S(1)}, bf16[768,256]{1,0:T(8,128)(2,1)}, u32[]{:S(2)}) copy-start(bf16[768,256]{1,0:T(8,128)(2,1)} %param.18) | copy-start | bytes 1179652
  233.4 174.8 %copy-start.11 = (f32[256]{0:T(256)S(1)}, f32[256]{0:T(256)}, u32[]{:S(2)}) copy-start(f32[256]{0:T(256)} %param.19) | copy-start | bytes 3076
Sparse Core Ops, SparseCore 0:
  46.8 346.1 all-reduce.1
where the time goes:
time: 417 us; the launch traced here: 416 us
  blocking collectives  188 us (45%)
  waiting for transfers between devices  160 us (38%)
  local copies, waits for them, and re-layouts  22.2 us (5%)
  starting transfers between devices  20.6 us (5%)
  between operations  13.8 us (3%)
  matrix products  8.32 us (2%)
    all_gather x1, blocking collectives, on_device(): hub_table = lax.all_gather(own_hubs, 'dom', axis=0, tiled=True)  160 us
    psum x1, waiting for transfers between devices, on_device(): summed = lax.psum(partial_hubs, 'dom')  160 us
    all_to_all x1, starting transfers between devices, on_device(): lax.all_to_all(outgoing, 'dom', split_axis=0, concat_axis=0, tiled=True)  20.6 us
    all_gather x1, blocking collectives, on_device(): lax.all_gather(features, 'feat', axis=1, tiled=True)  14.5 us
    all_gather x1, blocking collectives, on_device(): lax.all_gather(mean_rows, 'feat', axis=1, tiled=True)  14.1 us
    gather x1, local copies, waits for them, and re-layouts, on_device(): outgoing = jnp.take(features, cut_source[0], axis=0)  11.1 us
  transfers between devices with their start and end apart: 2, of which 1 were waited for; matrix products, arithmetic and copies ran while one was open for 4% of the time, Pallas kernels for 0%

commit v1 on v0

v1 whole, which is shorter than its diff:
```python
import jax
import jax.numpy as jnp
from jax import lax
from jax.sharding import PartitionSpec as P


def on_device(features, w_self, w_neigh, out_bias, degrees, tile_index, tile_mask, cut_source, cut_target,
              hub_local, hub_source, hub_target, mirror_source, mirror_target):
    bf16, f32 = jnp.bfloat16, jnp.float32
    nodes, columns = features.shape
    parts, cap = cut_source.shape[1:]
    tile = tile_mask.shape[2]
    blocks = nodes // tile
    hub_dev = hub_local.shape[1]
    hubs = parts * hub_dev
    node_ids = jnp.arange(nodes, dtype=jnp.int32)
    hub_ids = jnp.arange(hubs, dtype=jnp.int32)
    dot = lambda a, b: jnp.dot(a, b, preferred_element_type=f32)

    take_cut = (cut_source[0].reshape(-1)[:, None] == node_ids[None, :]).astype(bf16)
    outgoing = dot(take_cut, features).astype(bf16).reshape(parts, cap, columns)
    own_hubs = dot((hub_local[0][:, None] == node_ids[None, :]).astype(bf16), features).astype(bf16)
    mirror_to = (hub_ids[:, None] == mirror_target[0][None, :]).astype(bf16)
    mirror_from = (mirror_source[0][:, None] == node_ids[None, :]).astype(bf16)
    partial = dot(dot(mirror_to, mirror_from).astype(bf16), features).astype(bf16).reshape(parts, hub_dev, columns)
    message = jnp.concatenate(
        [outgoing, jnp.broadcast_to(own_hubs[None], (parts, hub_dev, columns)), partial], axis=1)
    arrived = lax.all_to_all(message, "dom", split_axis=0, concat_axis=0, tiled=True)
    all_features = lax.all_gather(features, "feat", axis=1, tiled=True)
    carry = dot(all_features, w_self)

    cut_to = (node_ids[:, None, None] == cut_target[0][None]).astype(bf16)
    hub_to = dot((node_ids[:, None] == hub_target[0][None, :]).astype(bf16),
                 (hub_source[0][:, None] == hub_ids[None, :]).astype(bf16)).astype(bf16).reshape(nodes, parts, hub_dev)
    master_to = jnp.broadcast_to((node_ids[:, None] == hub_local[0][None, :]).astype(bf16)[:, None], hub_to.shape)
    place = jnp.concatenate([cut_to, hub_to, master_to], axis=2).reshape(nodes, -1)

    row_is = (tile_index[0, :, 0][:, None] == jnp.arange(blocks)[None, :]).astype(f32)
    col_is = (tile_index[0, :, 1][:, None] == jnp.arange(blocks)[None, :]).astype(f32)
    adjacency = jnp.einsum("tr,tc,tuv->rucv", row_is, col_is, tile_mask[0].astype(f32)).reshape(nodes, nodes)
    total = dot(adjacency.astype(bf16), features) + dot(place, arrived.reshape(-1, columns))
    mean_rows = (total / degrees.astype(f32)[:, None]).astype(bf16)
    out = carry + dot(lax.all_gather(mean_rows, "feat", axis=1, tiled=True), w_neigh)
    return jax.nn.relu(out + out_bias[None, :]).astype(bf16)


def solution(mesh):
    return jax.shard_map(
        on_device,
        mesh=mesh,
        in_specs=(P("dom", "feat"), P(None, "feat"), P(None, "feat"), P("feat"), P("dom"), P("dom"), P("dom"), P("dom"),
                  P("dom"), P("dom"), P("dom"), P("dom"), P("dom"), P("dom")),
        out_specs=P("dom", "feat"),
        check_vma=False,
    )
```

time: 417 us -> 147 us (0.35)
  blocking collectives: 188 us -> 27.3 us
  waiting for transfers between devices: 160 us -> 78.1 us
  local copies, waits for them, and re-layouts: 22.2 us -> 4.14 us
  between operations: 13.8 us -> 0.26 us
  matrix products: 8.32 us -> 13.2 us
    all_gather x2 -> x1, blocking collectives: 174 us -> 13.9 us  [on_device(): all_features = lax.all_gather(features, 'feat', axis=1, tiled=True)]
    psum x1 -> x0, waiting for transfers between devices: 160 us -> none  [on_device(): summed = lax.psum(partial_hubs, 'dom')]
    all_to_all x1, waiting for transfers between devices: 0.01 us -> 78.1 us  [on_device(): lax.all_to_all(message, 'dom', split_axis=0, concat_axis=0, tiled=True)]
    gather x5 -> x0, local copies, waits for them, and re-layouts: 16.2 us -> none  [the longest x1 11.1 us: on_device(): outgoing = jnp.take(features, cut_source[0], axis=0)]
    dot_general x8 -> x9, matrix products: 8.32 us -> 13.2 us  [the longest x8 12.8 us: on_device(): dot = lambda a, b: jnp.dot(a, b, preferred_element_type=f32)]
  transfers between devices with their start and end apart: 2 -> 1, of which waited for: 1 -> 1; matrix products, arithmetic and copies ran while one was open for 4% -> 4% of each run, Pallas kernels for 0% -> 0%
where the time goes in v1:
time: 147 us
  waiting for transfers between devices  78.1 us (53%)
  blocking collectives  27.3 us (19%)
  starting transfers between devices  20.6 us (14%)
  matrix products  13.2 us (9%)
  local copies, waits for them, and re-layouts  4.14 us (3%)
  other arithmetic  3.01 us (2%)
    all_to_all x1, waiting for transfers between devices, on_device(): lax.all_to_all(message, 'dom', split_axis=0, concat_axis=0, tiled=True)  78.1 us
    all_to_all x1, starting transfers between devices, on_device(): lax.all_to_all(message, 'dom', split_axis=0, concat_axis=0, tiled=True)  20.6 us
    all_gather x1, blocking collectives, on_device(): all_features = lax.all_gather(features, 'feat', axis=1, tiled=True)  13.9 us
    all_gather x1, blocking collectives, on_device(): lax.all_gather(mean_rows, 'feat', axis=1, tiled=True)  13.4 us
    dot_general x8, matrix products, on_device(): dot = lambda a, b: jnp.dot(a, b, preferred_element_type=f32)  12.8 us
  transfers between devices with their start and end apart: 1, of which 1 were waited for; matrix products, arithmetic and copies ran while one was open for 4% of the time, Pallas kernels for 0%

profile of v1, /device:TPU:6, one launch (start us, length us, event | category | flops | bytes accessed | tf_op | source)
XLA Modules:
  0.0 146.6 jit_solution(10326353817390989338)
XLA Ops:
  0.0 0.0 copy-start
  0.0 1.9 %fusion.23 = bf16[512,192]{0,1:T(8,128)(2,1)S(1)} fusion(bf16[512,192]{0,1:T(8,128)(2,1)} %param.14, s32[512]{0:T(512)} %bitcast.45, s32[512]{0:T(512)} %bitcast.46), kind=kOutput, calls=%fused_computation.27 | convolution fusion | flops 369983488 | bytes 397312 | tf_op jit(solution)/shard_map/dot_general | solution.py:18
  1.9 0.1 copy.47
  2.0 0.1 reshape.44
  2.1 1.1 convolution_convert_fusion.3
  3.2 0.0 copy-done.7
  3.2 0.1 copy.45
  3.4 0.1 eq.176
  3.5 0.0 copy-done.3
  3.5 2.3 %fusion.8 = bf16[3072,192]{0,1:T(8,128)(2,1)S(1)} fusion(bf16[512,192]{0,1:T(8,128)(2,1)S(1)} %copy-done.3, s32[3072]{0:T(1024)S(1)} %eq.176), kind=kOutput, calls=%fused_computation.10 | convolution fusion | flops 606142464 | bytes 1388544 | tf_op jit(solution)/shard_map/dot_general | solution.py:18
  5.8 0.7 copy.46
  6.4 0.1 broadcast_in_dim.5
  6.5 2.1 %pad_maximum_fusion = bf16[128,32,192]{2,1,0:T(8,128)(2,1)} fusion(bf16[128,4,192]{2,1,0:T(4,128)(2,1)S(1)} %reshape.44, bf16[128,4,192]{2,1,0:T(4,128)(2,1)S(1)} %broadcast_in_dim.5, bf16[128,24,192]{2,1,0:T(8,128)(2,1)S(1)} %bitcast.40), kind=kLoop, calls=%fused_computation.12 | loop fusion | flops 4718592 | bytes 3145728 | tf_op jit(solution)/shard_map/concatenate | solution.py:26
  8.6 20.6 %all-to-all-start = ((bf16[128,32,192]{2,1,0:T(8,128)(2,1)}), bf16[128,32,192]{2,1,0:T(8,128)(2,1)}, u32[]{:S(2)}, u32[]{:S(2)}) async-start(bf16[128,32,192]{2,1,0:T(8,128)(2,1)} %pad_maximum_fusion), calls=%async_computation | async-start | bytes 4194304 | tf_op jit(solution)/shard_map/all_to_all | solution.py:28
  29.2 0.0 copy-done.12
  29.2 0.0 copy-done.13
  29.3 0.0 copy-start.8
  29.3 0.0 copy-start.10
  29.3 0.0 copy-start.4
  29.3 0.6 convolution_convert_fusion.2
  29.9 0.1 reshape.42
  30.0 1.2 copy.44
  31.2 0.0 copy-done.9
  31.2 0.0 copy-done.1
  31.2 0.1 convert_bitcast_fusion
  31.3 0.4 fusion.14
  31.7 1.2 copy.43
  32.9 0.0 copy-done.8
  32.9 0.0 copy-done.10
  32.9 0.1 fusion.36
  33.0 0.0 copy-done.4
  33.0 13.9 %all_gather.6 = bf16[512,768]{0,1:T(8,128)(2,1)S(1)} all-gather(bf16[512,192]{0,1:T(8,128)(2,1)S(1)} %copy-done.4), channel_id=1, replica_groups=mesh['dom'=128,'feat'=4] {'feat'}, dimensions={1}, use_global_device_ids=true | all-gather | bytes 983040 | tf_op jit(solution)/shard_map/all_gather | solution.py:29
  46.9 0.0 copy-done
  46.9 1.2 fusion.43
  48.1 0.0 copy-done.6
  48.1 0.8 fusion
  48.9 78.1 %all-to-all-done = bf16[128,32,192]{2,1,0:T(8,128)(2,1)} async-done(((bf16[128,32,192]{2,1,0:T(8,128)(2,1)}), bf16[128,32,192]{2,1,0:T(8,128)(2,1)}, u32[]{:S(2)}, u32[]{:S(2)}) %all-to-all-start) | async-done | bytes 1572896 | tf_op jit(solution)/shard_map/all_to_all | solution.py:28
  127.0 0.3 broadcast_in_dim.4
  127.4 0.0 copy-start.2
  127.4 0.0 copy-start.5
  127.4 4.3 %fusion.16 = f32[512,192]{0,1:T(8,128)S(1)} fusion(bf16[128,32,192]{2,1,0:T(8,128)(2,1)} %all-to-all-done, bf16[512,128,4]{1,0,2:T(8,128)(2,1)S(1)} %broadcast_in_dim.4, bf16[512,128,4]{1,0,2:T(8,128)(2,1)} %copy.44, bf16[512,128,24]{1,0,2:T(8,128)(2,1)S(1)} %fusion), kind=kOutput, calls=%fused_computation.23 | convolution fusion | flops 809500672 | bytes 6160384 | tf_op jit(solution)/shard_map/dot_general | solution.py:18
  131.7 0.0 copy-start.11
  131.7 0.0 copy-start.14
  131.7 0.0 copy-start.15
  131.7 0.0 copy-done.2
  131.7 0.3 fusion.22
  132.1 13.4 %all_gather.7 = bf16[512,768]{0,1:T(8,128)(2,1)S(1)} all-gather(bf16[512,192]{0,1:T(8,128)(2,1)S(1)} %fusion.22), channel_id=1, replica_groups=mesh['dom'=128,'feat'=4] {'feat'}, dimensions={1}, use_global_device_ids=true | all-gather | bytes 983040 | tf_op jit(solution)/shard_map/all_gather | solution.py:43
  145.5 1.1 fusion.15
  (14 shorter events, 0.0 us)
Async XLA Ops:
  0.0 46.9 %copy-start = (bf16[768,256]{1,0:T(8,128)(2,1)S(1)}, bf16[768,256]{1,0:T(8,128)(2,1)}, u32[]{:S(2)}) copy-start(bf16[768,256]{1,0:T(8,128)(2,1)} %param.15) | copy-start | bytes 1179652
  0.0 3.5 %copy-start.3 = (bf16[512,192]{0,1:T(8,128)(2,1)S(1)}, bf16[512,192]{0,1:T(8,128)(2,1)}, u32[]{:S(2)}) copy-start(bf16[512,192]{0,1:T(8,128)(2,1)} %param.14) | copy-start | bytes 589828
  0.0 3.2 %copy-start.7 = (s32[1,128,24]{1,2,0:T(8,128)S(1)}, s32[1,128,24]{1,2,0:T(8,128)}, u32[]{:S(2)}) copy-start(s32[1,128,24]{1,2,0:T(8,128)} %param.21) | copy-start | bytes 36868
  8.6 20.6 %copy-start.12 = (s32[1,512]{1,0:T(1,128)S(1)}, s32[1,512]{1,0:T(1,128)}, u32[]{:S(2)}) copy-start(s32[1,512]{1,0:T(1,128)} %param.24) | copy-start | bytes 6148
  8.6 20.6 %copy-start.13 = (s32[1,512]{1,0:T(1,128)S(1)}, s32[1,512]{1,0:T(1,128)}, u32[]{:S(2)}) copy-start(s32[1,512]{1,0:T(1,128)} %param.25) | copy-start | bytes 6148
  8.6 22.6 %copy-start.9 = (s32[1,12,2]{1,2,0:T(2,128)S(1)}, s32[1,12,2]{1,2,0:T(2,128)}, u32[]{:S(2)}) copy-start(s32[1,12,2]{1,2,0:T(2,128)} %param.19) | copy-start | bytes 292
  8.6 22.6 %copy-start.1 = (s32[1,12,128,128]{3,2,1,0:T(8,128)S(1)}, s32[1,12,128,128]{3,2,1,0:T(8,128)}, u32[]{:S(2)}) copy-start(s32[1,12,128,128]{3,2,1,0:T(8,128)} %param.20) | copy-start | bytes 2359300
  8.6 118.4 %all-to-all-start = ((bf16[128,32,192]{2,1,0:T(8,128)(2,1)}), bf16[128,32,192]{2,1,0:T(8,128)(2,1)}, u32[]{:S(2)}, u32[]{:S(2)}) async-start(bf16[128,32,192]{2,1,0:T(8,128)(2,1)} %pad_maximum_fusion), calls=%async_computation | async-start | bytes 4194304 | tf_op jit(solution)/shard_map/all_to_all | solution.py:28
  29.3 3.7 %copy-start.8 = (s32[512]{0:T(512)S(1)}, s32[512]{0:T(512)}, u32[]{:S(2)}) copy-start(s32[512]{0:T(512)} %param.18) | copy-start | bytes 6148
  29.3 3.7 %copy-start.10 = (s32[1,4]{1,0:T(1,128)S(1)}, s32[1,4]{1,0:T(1,128)}, u32[]{:S(2)}) copy-start(s32[1,4]{1,0:T(1,128)} %param.23) | copy-start | bytes 52
  29.3 3.7 %copy-start.4 = (bf16[512,192]{0,1:T(8,128)(2,1)S(1)}, bf16[512,192]{0,1:T(8,128)(2,1)}, u32[]{:S(2)}) copy-start(bf16[512,192]{0,1:T(8,128)(2,1)} %param.14) | copy-start | bytes 589828
  31.2 16.9 %copy-start.6 = (s32[1,128,24]{1,2,0:T(8,128)S(1)}, s32[1,128,24]{1,2,0:T(8,128)}, u32[]{:S(2)}) copy-start(s32[1,128,24]{1,2,0:T(8,128)} %param.22) | copy-start | bytes 36868
  127.4 4.3 %copy-start.2 = (bf16[4,128,4,128]{3,2,1,0:T(4,128)(2,1)S(1)}, bf16[4,128,4,128]{3,2,1,0:T(4,128)(2,1)}, u32[]{:S(2)}) copy-start(bf16[4,128,4,128]{3,2,1,0:T(4,128)(2,1)} %copy.43) | copy-start | bytes 1572868
  127.4 4.3 %copy-start.5 = (bf16[512,192]{0,1:T(8,128)(2,1)S(1)}, bf16[512,192]{0,1:T(8,128)(2,1)}, u32[]{:S(2)}) copy-start(bf16[512,192]{0,1:T(8,128)(2,1)} %param.14) | copy-start | bytes 589828
  131.7 13.8 %copy-start.11 = (bf16[768,256]{1,0:T(8,128)(2,1)S(1)}, bf16[768,256]{1,0:T(8,128)(2,1)}, u32[]{:S(2)}) copy-start(bf16[768,256]{1,0:T(8,128)(2,1)} %param.16) | copy-start | bytes 1179652
  131.7 13.8 %copy-start.14 = (f32[256]{0:T(256)S(1)}, f32[256]{0:T(256)}, u32[]{:S(2)}) copy-start(f32[256]{0:T(256)} %param.17) | copy-start | bytes 3076
  131.7 13.8 %copy-start.15 = (f32[512,256]{1,0:T(8,128)S(1)}, f32[512,256]{1,0:T(8,128)}, u32[]{:S(2)}) copy-start(f32[512,256]{1,0:T(8,128)} %fusion.43) | copy-start | bytes 1572868

commit v2 on v1

v2 whole, which is shorter than its diff:
```python
import functools

import jax
import jax.numpy as jnp
from jax import lax
from jax.experimental import pallas as pl
from jax.experimental.pallas import tpu as pltpu
from jax.sharding import PartitionSpec as P

MESH = pl.DeviceIdType.MESH
BF16, F32, I32 = jnp.bfloat16, jnp.float32, jnp.int32
PLANE = 8
SLOTS = 32
ROWS = 816
PIECES, PIECE = 3, 272
CUT = 416
SHIFT = 256


def dot(a, b):
    return jnp.dot(a, b, preferred_element_type=F32)


def dot_nt(a, b):
    return lax.dot_general(a, b, (((1,), (1,)), ((), ())), preferred_element_type=F32)


def iota(shape, axis):
    return lax.broadcasted_iota(I32, shape, axis)


def hot(mask):
    return jnp.where(mask, 1.0, 0.0).astype(BF16)


def column(row):
    return jnp.transpose(jnp.broadcast_to(row, (128, 128)))


def kernel(rings, feats, item, feat, tidx, tgt, hub_at, hub_t, hub_s, deg, bias, mask_hbm, ws_hbm, wn_hbm, out,
           ring, ysend, yrecv, xf, xm, accp, accm, accl, msum, hub_hot, mask, ws, wn, wfold, carry,
           zs, zr, ys, yr, fs, fr, ms, mr, local):
    half = rings // 2
    dom, x = lax.axis_index("dom"), lax.axis_index("feat")
    z, me = dom // PLANE, dom % PLANE
    up, down = ((z + 1) % rings) * PLANE + me, ((z + rings - 1) % rings) * PLANE + me

    loads = [pltpu.make_async_copy(src, dst, local.at[i])
             for i, (src, dst) in enumerate(((mask_hbm, mask), (ws_hbm, ws), (wn_hbm, wn)))]
    for load in loads:
        load.start()

    barrier = pltpu.get_barrier_semaphore()
    for dev in (up, down):
        pl.semaphore_signal(barrier, inc=1, device_id=(dev, x), device_id_type=MESH)
    for o in range(1, PLANE):
        pl.semaphore_signal(barrier, inc=1, device_id=(z * PLANE + (me + o) % PLANE, x), device_id_type=MESH)
    for o in range(1, feats):
        pl.semaphore_signal(barrier, inc=1, device_id=(dom, (x + o) % feats), device_id_type=MESH)
    pl.semaphore_wait(barrier, 2 + PLANE - 1 + feats - 1)

    def zcopy(way, step, piece, src):
        slot = (z + rings - step) % rings if way == 0 else (z + step) % rings
        rows = pl.ds(piece * PIECE, PIECE)
        return pltpu.make_async_remote_copy(
            src_ref=src.at[rows] if src is not None else ring.at[slot, rows], dst_ref=ring.at[slot, rows],
            send_sem=zs.at[way, step, piece], recv_sem=zr.at[slot, piece],
            device_id=(up if way == 0 else down, x), device_id_type=MESH)

    def zlast(way):
        step = half - 1
        slot = (z + rings - step) % rings if way == 0 else (z + step) % rings
        rows = pl.ds(0, CUT) if way == 0 else pl.ds(CUT, ROWS - CUT)
        return pltpu.make_async_remote_copy(
            src_ref=ring.at[slot, rows], dst_ref=ring.at[slot, rows],
            send_sem=zs.at[way, step, 0], recv_sem=zr.at[slot, way],
            device_id=(up if way == 0 else down, x), device_id_type=MESH)

    def zarrived(way, step, piece):
        slot = (z + rings - step) % rings if way == 0 else (z + step) % rings
        rows = pl.ds(piece * PIECE, PIECE)
        pltpu.make_async_remote_copy(
            src_ref=ring.at[slot, rows], dst_ref=ring.at[slot, rows], send_sem=zs.at[way, 0, piece],
            recv_sem=zr.at[slot, piece], device_id=(up, x), device_id_type=MESH).wait_recv()

    def zlast_arrived(way):
        slot = (z + half) % rings
        rows = pl.ds(0, CUT) if way == 0 else pl.ds(CUT, ROWS - CUT)
        pltpu.make_async_remote_copy(
            src_ref=ring.at[slot, rows], dst_ref=ring.at[slot, rows], send_sem=zs.at[way, 0, 0],
            recv_sem=zr.at[slot, way], device_id=(up, x), device_id_type=MESH).wait_recv()

    def ycopy(step, o, rows):
        dest = (me + o) % PLANE
        return pltpu.make_async_remote_copy(
            src_ref=ysend.at[step, dest, pl.ds(0, rows)], dst_ref=yrecv.at[step, me, pl.ds(0, rows)],
            send_sem=ys.at[step, o - 1], recv_sem=yr.at[step, me],
            device_id=(z * PLANE + dest, x), device_id_type=MESH)

    def yarrived(step, rows):
        for o in range(1, PLANE):
            src = (me + o) % PLANE
            pltpu.make_async_remote_copy(
                src_ref=ysend.at[step, src, pl.ds(0, rows)], dst_ref=yrecv.at[step, src, pl.ds(0, rows)],
                send_sem=ys.at[step, o - 1], recv_sem=yr.at[step, src],
                device_id=(z * PLANE + src, x), device_id_type=MESH).wait_recv()

    def xcopy(buf, send, recv, o):
        return pltpu.make_async_remote_copy(
            src_ref=buf.at[x], dst_ref=buf.at[x], send_sem=send.at[o - 1], recv_sem=recv.at[x],
            device_id=(dom, (x + o) % feats), device_id_type=MESH)

    def xarrived(buf, send, recv, o):
        src = (x + o) % feats
        pltpu.make_async_remote_copy(
            src_ref=buf.at[src], dst_ref=buf.at[src], send_sem=send.at[o - 1], recv_sem=recv.at[src],
            device_id=(dom, src), device_id_type=MESH).wait_recv()

    def select(ref):
        ids = ref[768:800, :].astype(F32)
        row = iota((32, 128), 0)
        cols = [column(jnp.sum(jnp.where(row == 2 * z + i, ids, 0.0), axis=0, keepdims=True)) for i in (0, 1)]
        lane = iota((128, 128), 1).astype(F32) - SHIFT
        blocks = [jnp.concatenate([hot(c == lane + 128.0 * b) for c in cols], axis=0) for b in range(4)]
        edges = ref[800:816, :].astype(F32)
        hub = (iota((32, 128), 0) + z * 32 - SHIFT).astype(F32)
        node = (iota((512, 128), 0) - SHIFT).astype(F32)
        to = jnp.concatenate([hot(hub == edges[4 + c:5 + c, :]) for c in range(4)], axis=1)
        fro = jnp.concatenate([hot(node == edges[c:c + 1, :]) for c in range(4)], axis=1)
        count = dot_nt(to, fro).astype(BF16)
        fold = ref[512:768, :]
        got = []
        for i in (0, 1):
            left = jnp.concatenate(
                [jnp.concatenate(blocks[2 * i:2 * i + 2], axis=1), count[:, 256 * i:256 * i + 256]], axis=0)
            right = jnp.concatenate([ref[256 * i:256 * i + 256, :], fold], axis=1)
            part = dot(left, right)
            msum[i] += part[256:288, :]
            got.append(part[:256, :])
        return got

    low = iota((256, 128), 1) < 64

    def put(step, way, got):
        ysend[step, :, 64 * way:64 * way + 32, :] = (got[0][:, :128] + got[1][:, :128]).astype(BF16).reshape(
            PLANE, SLOTS, 128)
        if way == 0:
            tail = jnp.where(low, got[0][:, 128:] + pltpu.roll(got[1][:, 128:], 64, 1), 0.0)
        else:
            before = ysend[step, :, 32:64, :].reshape(256, 128).astype(F32)
            tail = jnp.where(low, before, got[1][:, 128:] + pltpu.roll(got[0][:, 128:], 64, 1))
        ysend[step, :, 32:64, :] = tail.astype(BF16).reshape(PLANE, SLOTS, 128)

    def send(step, rows):
        for o in (4, 5, 3, 2, 6, 1, 7):
            ycopy(step, o, rows).start()
        yrecv[step, me, 0:rows, :] = ysend[step, me, 0:rows, :]

    def place(step, way, last=False):
        zz = (z + rings - step) % rings if way == 0 else (z + step) % rings
        to = tgt[zz]
        if last:
            to = jnp.where((iota((1, 256), 1) % SLOTS) >= 28, hub_at[...], to)
        node = iota((512, 256), 0)
        pos = iota((256, 512), 0)
        slot = pos % SLOTS
        hub = jnp.where((slot >= 24) & (slot < 28), zz * 32 + (pos // SLOTS) * 4 + slot - 24, -1)
        where = dot_nt(hub_hot[...], hot(hub == hub_s[...]))
        where = (where + jnp.where(node == to, 1.0, 0.0)).astype(BF16)
        rows = jnp.concatenate([yrecv[step, :, 64 * way:64 * way + 32, :].reshape(256, 128),
                                yrecv[step, :, 32:64, :].reshape(256, 128)], axis=1)
        acc = accp if way == 0 else accm
        acc[...] += dot(where, rows)

    def product(buf, which):
        tops = bots = None
        for i in range(feats):
            fold = buf[i, 512:768, :]
            top = dot(jnp.concatenate([buf[i, 0:256, :], fold], axis=1), wfold[which, i, 0])
            bot = dot(jnp.concatenate([buf[i, 256:512, :], fold], axis=1), wfold[which, i, 1])
            tops, bots = (top, bot) if tops is None else (tops + top, bots + bot)
        return tops, bots

    for piece in range(PIECES):
        zcopy(0, 0, piece, item).start()
        zcopy(1, 0, piece, item).start()
    xf[x] = item[0:768, :]
    for o in range(1, feats):
        xcopy(xf, fs, fr, o).start()

    accp[...] = jnp.zeros_like(accp)
    accm[...] = jnp.zeros_like(accm)
    accl[...] = jnp.zeros_like(accl)
    msum[...] = jnp.zeros_like(msum)
    hub_hot[...] = hot(iota((512, 512), 0) == hub_t[...])

    ysend[0, :, 64:96, :] = jnp.zeros((PLANE, SLOTS, 128), BF16)
    put(0, 0, select(item))
    send(0, 96)

    for piece in range(PIECES):
        for way in (0, 1):
            zarrived(way, 1, piece)
            if half > 2:
                zcopy(way, 1, piece, None).start()
    if half == 2:
        zlast(0).start()
        zlast(1).start()

    for load in loads:
        load.wait()

    def tile(t, _):
        at = tidx[pl.ds(t, 1), :]
        is_at = [[(at[:, i:i + 1] == b).astype(F32) for b in range(4)] for i in (0, 1)]
        block = sum(feat[128 * b:128 * b + 128, :].astype(F32) * is_at[1][b] for b in range(4)).astype(BF16)
        part = dot(mask[t].astype(F32).astype(BF16), block)
        for b in range(4):
            accl[128 * b:128 * b + 128, 0:192] += part * is_at[0][b]
        return 0

    lax.fori_loop(0, 12, tile, 0)

    for which, w in enumerate((ws, wn)):
        for i in range(feats):
            a, b, zero = w[192 * i:192 * i + 128, :], w[192 * i + 128:192 * i + 192, :], jnp.zeros((64, 256), BF16)
            wfold[which, i, 0] = jnp.concatenate([a, b, zero], axis=0)
            wfold[which, i, 1] = jnp.concatenate([a, zero, b], axis=0)

    def step(k, _):
        for way in (0, 1):
            zarrived(way, k, 0)
            zcopy(way, k, 0, None).start()
        put(k - 1, 0, select(ring.at[(z + rings - k + 1) % rings]))
        for way in (0, 1):
            zarrived(way, k, 1)
            zcopy(way, k, 1, None).start()
        put(k - 1, 1, select(ring.at[(z + k - 1) % rings]))
        send(k - 1, 96)
        for way in (0, 1):
            zarrived(way, k, 2)
            zcopy(way, k, 2, None).start()
        yarrived(k - 2, 96)
        place(k - 2, 0)
        place(k - 2, 1)
        return 0

    lax.fori_loop(2, half - 1, step, 0)
    k = half - 1
    if half > 2:
        for way in (0, 1):
            zarrived(way, k, 0)
            zarrived(way, k, 1)
        zlast(0).start()
        for way in (0, 1):
            zarrived(way, k, 2)
        zlast(1).start()
        put(k - 1, 0, select(ring.at[(z + rings - k + 1) % rings]))
        put(k - 1, 1, select(ring.at[(z + k - 1) % rings]))
        send(k - 1, 96)
    put(k, 0, select(ring.at[(z + rings - k) % rings]))
    put(k, 1, select(ring.at[(z + k) % rings]))
    send(k, 96)
    if half > 2:
        yarrived(k - 2, 96)
        place(k - 2, 0)
        place(k - 2, 1)
    yarrived(k - 1, 96)
    place(k - 1, 0)
    place(k - 1, 1)
    for o in range(1, feats):
        xarrived(xf, fs, fr, o)
    top, bot = product(xf, 0)
    carry[0:256, :] = top + bias[...]
    carry[256:512, :] = bot + bias[...]

    zlast_arrived(0)
    zlast_arrived(1)
    got = select(ring.at[(z + half) % rings])
    row, col = iota((256, 32), 0), iota((256, 32), 1)
    spread = hot((row // SLOTS == col // 4) & (row % SLOTS == 28 + col % 4))
    got = [part + dot(spread, msum[i].astype(BF16)) for i, part in enumerate(got)]
    put(half, 0, got)
    send(half, 64)
    yarrived(k, 96)
    place(k, 0)
    place(k, 1)
    yarrived(half, 64)
    place(half, 0, last=True)

    degree = deg[...].astype(F32)
    degree = jnp.concatenate([column(degree[i:i + 1, :]) for i in range(4)], axis=0)
    lead = (accp[:, 0:128] + accm[:, 0:128] + accl[:, 0:128]) / degree
    rest = (accp[:, 128:256] + pltpu.roll(accm[:, 128:256], 64, 1) + accl[:, 128:256]) / degree
    xm[x, 0:512, :] = lead.astype(BF16)
    xm[x, 512:768, :] = jnp.where(low, rest[0:256, :], pltpu.roll(rest[256:512, :], 64, 1)).astype(BF16)
    for o in range(1, feats):
        xcopy(xm, ms, mr, o).start()
    for o in range(1, feats):
        xarrived(xm, ms, mr, o)
    top, bot = product(xm, 1)
    out[0:256, :] = jnp.maximum(carry[0:256, :] + top, 0.0).astype(BF16)
    out[256:512, :] = jnp.maximum(carry[256:512, :] + bot, 0.0).astype(BF16)

    for way in (0, 1):
        for s in range(half - 1):
            for piece in range(PIECES):
                zcopy(way, s, piece, item if s == 0 else None).wait_send()
        zlast(way).wait_send()
    for o in range(1, PLANE):
        for s in range(half):
            ycopy(s, o, 96).wait_send()
        ycopy(half, o, 64).wait_send()
    for o in range(1, feats):
        xcopy(xf, fs, fr, o).wait_send()
        xcopy(xm, ms, mr, o).wait_send()


def on_device(rings, feats, features, w_self, w_neigh, out_bias, degrees, tile_index, tile_mask, cut_source, cut_target,
              hub_local, hub_source, hub_target, mirror_source, mirror_target):
    parts = rings * PLANE
    half = rings // 2
    fold = jnp.concatenate([features[0:256, 128:], features[256:, 128:]], axis=1)
    ids = jnp.concatenate([cut_source[0], jnp.broadcast_to(hub_local, (parts, 4)), jnp.full((parts, 4), 640, I32)], axis=1)
    ids = jnp.concatenate([ids.reshape(-1, 128), jnp.full((32 - parts // 4, 128), 640, I32),
                           mirror_source.reshape(4, 128), mirror_target.reshape(4, 128), jnp.full((8, 128), 640, I32)], axis=0)
    item = jnp.concatenate([features[:, :128], fold, (ids - SHIFT).astype(BF16)], axis=0)
    tgt = jnp.concatenate([cut_target[0], jnp.full((parts, 8), -1, I32)], axis=1).reshape(rings, 1, 256)
    hub_at = jnp.tile(jnp.tile(hub_local, (1, 8)), (1, PLANE))
    vmem, anywhere = pl.BlockSpec(memory_space=pltpu.VMEM), pl.BlockSpec(memory_space=pl.ANY)
    return pl.pallas_call(
        functools.partial(kernel, rings, feats),
        out_shape=jax.ShapeDtypeStruct((512, 256), BF16),
        in_specs=[vmem] * 9 + [anywhere] * 3,
        out_specs=vmem,
        scratch_shapes=[
            pltpu.VMEM((rings, ROWS, 128), BF16),
            pltpu.VMEM((half + 1, PLANE, 96, 128), BF16),
            pltpu.VMEM((half + 1, PLANE, 96, 128), BF16),
            pltpu.VMEM((feats, 768, 128), BF16),
            pltpu.VMEM((feats, 768, 128), BF16),
            pltpu.VMEM((512, 256), F32),
            pltpu.VMEM((512, 256), F32),
            pltpu.VMEM((512, 256), F32),
            pltpu.VMEM((2, 32, 256), F32),
            pltpu.VMEM((512, 512), BF16),
            pltpu.VMEM((12, 128, 128), I32),
            pltpu.VMEM((192 * feats, 256), BF16),
            pltpu.VMEM((192 * feats, 256), BF16),
            pltpu.VMEM((2, feats, 2, 256, 256), BF16),
            pltpu.VMEM((512, 256), F32),
            pltpu.SemaphoreType.DMA((2, half, PIECES)),
            pltpu.SemaphoreType.DMA((rings, PIECES)),
            pltpu.SemaphoreType.DMA((half + 1, PLANE)),
            pltpu.SemaphoreType.DMA((half + 1, PLANE)),
            pltpu.SemaphoreType.DMA((4,)),
            pltpu.SemaphoreType.DMA((4,)),
            pltpu.SemaphoreType.DMA((4,)),
            pltpu.SemaphoreType.DMA((4,)),
            pltpu.SemaphoreType.DMA((3,)),
        ],
        compiler_params=pltpu.CompilerParams(
            collective_id=0, has_side_effects=True, vmem_limit_bytes=40 * 1024 * 1024),
        cost_estimate=pl.CostEstimate(flops=10**10, bytes_accessed=4 * 10**6, transcendentals=0),
    )(item, features, tile_index[0], tgt, hub_at, hub_target, hub_source, degrees.reshape(4, 128), out_bias.reshape(1, 256),
      tile_mask[0], w_self, w_neigh)


def solution(mesh):
    return jax.shard_map(
        functools.partial(on_device, mesh.shape["dom"] // PLANE, mesh.shape["feat"]),
        mesh=mesh,
        in_specs=(P("dom", "feat"), P(None, "feat"), P(None, "feat"), P("feat"), P("dom"), P("dom"), P("dom"), P("dom"),
                  P("dom"), P("dom"), P("dom"), P("dom"), P("dom"), P("dom")),
        out_specs=P("dom", "feat"),
        check_vma=False,
    )
```

time: 147 us -> 83.5 us (0.57)
  the two profiles are of different devices: /device:TPU:6 before, /device:TPU:1 now
where the time goes in v2:
time: 83.5 us; the launch traced here: 83.3 us
  Pallas kernels  75.4 us (90%)
  local copies, waits for them, and re-layouts  7.5 us (9%)
    pallas_call x1, Pallas kernels, on_device(): pl.pallas_call(functools.partial(kernel, rings, feats), out_shape=jax.Sha...  75.4 us
    unnamed x33, local copies, waits for them, and re-layouts  6.71 us

profile of v2, /device:TPU:1, one launch (start us, length us, event | category | flops | bytes accessed | tf_op | source)
XLA Modules:
  0.0 83.3 jit_solution(10042716325909399703)
XLA Ops:
  0.0 0.0 copy-start.2
  0.0 1.1 %copy.22.feat = bf16[512,192]{1,0:T(8,128)(2,1)S(1)} copy(bf16[512,192]{0,1:T(8,128)(2,1)} %param.14) | data formatting | bytes 393216 | tf_op args[0]
  1.1 0.0 copy-start
  1.2 0.7 copy-done
  1.8 0.0 copy-start.14
  1.8 0.0 copy-start.10
  1.9 0.0 slice-start
  1.9 0.6 copy-done.14
  2.5 0.1 pad.10.clone
  2.6 0.1 pad.11.clone
  2.7 0.0 copy-done.10
  2.7 0.1 add_add_fusion.1
  2.7 0.1 copy.25
  2.8 0.1 reshape.29
  2.9 0.0 copy-start.12
  2.9 0.1 pad.8.clone
  3.0 0.0 copy-start.11
  3.0 0.6 copy-done.12
  3.6 0.1 copy-done.11
  3.7 0.1 fusion
  3.8 0.0 slice-done
  3.8 0.0 copy-start.9
  3.8 0.0 copy-start.3
  3.8 0.1 pad_maximum_fusion.item
  3.9 0.0 copy-start.1
  3.9 0.1 tile.17
  4.0 0.1 tile.19.hub_at
  4.1 0.4 copy-done.9
  4.5 0.1 copy.30
  4.6 0.0 copy-start.6
  4.6 0.0 copy-start.7
  4.6 0.1 reshape.35.tgt
  4.7 0.0 copy-start.13
  4.7 0.7 copy-done.13
  5.4 0.1 copy.28.tidx
  5.5 0.0 copy-start.5
  5.5 0.0 copy-start.8
  5.5 0.0 copy-done.2
  5.5 0.0 copy-done.3
  5.5 0.0 copy-done.1
  5.5 0.0 copy-done.6
  5.5 0.0 copy-done.7
  5.5 0.6 copy-done.5
  6.2 0.0 copy-done.8
  6.2 0.0 copy-start.4
  6.2 1.0 %copy-done.4 = bf16[768,256]{1,0:T(8,128)(2,1)S(1)} copy-done((bf16[768,256]{1,0:T(8,128)(2,1)S(1)}, bf16[768,256]{1,0:T(8,128)(2,1)}, u32[]{:S(2)}) %copy-start.4) | copy-done | bytes 393240
  7.2 75.4 %shard_map.136 = bf16[512,256]{1,0:T(8,128)(2,1)S(1)} custom-call(bf16[816,128]{1,0:T(8,128)(2,1)S(1)} %pad_maximum_fusion.item, bf16[512,192]{1,0:T(8,128)(2,1)S(1)} %copy-done.1, s32[12,2]{1,0:T(8,128)S(1)} %copy.28.tidx, s32[16,1,256]{2,1,0:T(1,128)S(1)} %reshape.35.tgt, s32[1,256]{1,0:T(1,128)S(1)} %tile.19.hub_at, s32[1,512]{1,0:T(1,128)S(1)} %copy-done.5, ...), custom_call_target="tpu_custom_call" | custom-call | flops 10000000000 | bytes 4000000 | tf_op jit(solution)/shard_map/pallas_call | solution.py:331
  82.6 0.7 copy.32
  (6 shorter events, 0.0 us)
Async XLA Ops:
  0.0 5.5 %copy-start.2 = (s32[1,12,128,128]{3,2,1,0:T(8,128)S(1)}, s32[1,12,128,128]{3,2,1,0:T(8,128)}, u32[]{:S(2)}) copy-start(s32[1,12,128,128]{3,2,1,0:T(8,128)} %param.20) | copy-start | bytes 2359300
  1.1 0.7 copy-start
  1.8 0.7 copy-start.14
  1.8 0.8 copy-start.10
  1.9 1.9 %slice-start = ((bf16[512,192]{1,0:T(8,128)(2,1)}), bf16[512,128]{1,0:T(8,128)(2,1)S(1)}, s32[]{:S(2)}) async-start(bf16[512,192]{1,0:T(8,128)(2,1)} %copy-done), calls=%async_computation | async-start | bytes 262144 | tf_op jit(solution)/shard_map/slice | solution.py:327
  2.9 0.7 copy-start.12
  3.0 0.7 copy-start.11
  3.8 0.7 copy-start.9
  3.8 1.7 %copy-start.3 = (bf16[768,256]{1,0:T(8,128)(2,1)S(1)}, bf16[768,256]{1,0:T(8,128)(2,1)}, u32[]{:S(2)}) copy-start(bf16[768,256]{1,0:T(8,128)(2,1)} %ws_hbm.1) | copy-start | bytes 1179652
  3.9 1.6 %copy-start.1 = (bf16[512,192]{1,0:T(8,128)(2,1)S(1)}, bf16[512,192]{1,0:T(8,128)(2,1)}, u32[]{:S(2)}) copy-start(bf16[512,192]{1,0:T(8,128)(2,1)} %copy-done) | copy-start | bytes 589828
  4.6 0.9 %copy-start.6 = (s32[1,512]{1,0:T(1,128)S(1)}, s32[1,512]{1,0:T(1,128)}, u32[]{:S(2)}) copy-start(s32[1,512]{1,0:T(1,128)} %hub_s.1) | copy-start | bytes 6148
  4.6 0.9 %copy-start.7 = (s32[512]{0:T(512)S(1)}, s32[512]{0:T(512)}, u32[]{:S(2)}) copy-start(s32[512]{0:T(512)} %param.18) | copy-start | bytes 6148
  4.7 0.7 copy-start.13
  5.5 0.7 copy-start.5
  5.5 0.7 copy-start.8
  6.2 1.0 %copy-start.4 = (bf16[768,256]{1,0:T(8,128)(2,1)S(1)}, bf16[768,256]{1,0:T(8,128)(2,1)}, u32[]{:S(2)}) copy-start(bf16[768,256]{1,0:T(8,128)(2,1)} %wn_hbm.1) | copy-start | bytes 1179652

commit v3 on v1

v3 whole, which is shorter than its diff:
```python
import functools

import jax
import jax.numpy as jnp
from jax import lax
from jax.experimental import pallas as pl
from jax.experimental.pallas import tpu as pltpu
from jax.sharding import PartitionSpec as P

MESH = pl.DeviceIdType.MESH
BF16, F32, I32 = jnp.bfloat16, jnp.float32, jnp.int32
PLANE = 8
SLOTS = 32
WIDTH = 192
PIECES, PIECE = 6, 32
IDS = 48
SHIFT = 256


def dot(a, b):
    return jnp.dot(a, b, preferred_element_type=F32)


def dot_nt(a, b):
    return lax.dot_general(a, b, (((1,), (1,)), ((), ())), preferred_element_type=F32)


def iota(shape, axis):
    return lax.broadcasted_iota(I32, shape, axis)


def hot(mask):
    return jnp.where(mask, 1.0, 0.0).astype(BF16)


def column(row):
    return jnp.transpose(jnp.broadcast_to(row, (128, 128)))


def dot_tn(a, b):
    return lax.dot_general(a, b, (((0,), (0,)), ((), ())), preferred_element_type=F32)


def kernel(rings, feats, ft_hbm, cs_hbm, ct_hbm, ti_hbm, hl_hbm, ht_hbm, hs_hbm, mf_hbm, mt_hbm, deg_hbm, bias_hbm,
           mask_hbm, ws_hbm, wn_hbm, out, ring, ringi, ysend, yrecv, xf, xm, accp, accm, accl, msum, hub_hot, wfold, carry,
           own, tgt, raw, ft, cs, ct, tidx, hub_local, hub_t, hub_s, mirror_f, mirror_t, deg, bias, mask, ws, wn,
           zs, zr, ys, yr, fs, fr, ms, mr, local):
    half = rings // 2
    dom, x = lax.axis_index("dom"), lax.axis_index("feat")
    z, me = dom // PLANE, dom % PLANE
    up, down = ((z + 1) % rings) * PLANE + me, ((z + rings - 1) % rings) * PLANE + me

    barrier = pltpu.get_barrier_semaphore()
    for dev in (up, down):
        pl.semaphore_signal(barrier, inc=1, device_id=(dev, x), device_id_type=MESH)
    for o in range(1, PLANE):
        pl.semaphore_signal(barrier, inc=1, device_id=(z * PLANE + (me + o) % PLANE, x), device_id_type=MESH)
    for o in range(1, feats):
        pl.semaphore_signal(barrier, inc=1, device_id=(dom, (x + o) % feats), device_id_type=MESH)

    loads = [pltpu.make_async_copy(src, dst, local.at[i]) for i, (src, dst) in enumerate((
        (cs_hbm, cs), (hl_hbm, hub_local), (mf_hbm, mirror_f), (mt_hbm, mirror_t), (ft_hbm, ft), (ct_hbm, ct), (ti_hbm, tidx),
        (ht_hbm, hub_t), (hs_hbm, hub_s), (deg_hbm, deg), (bias_hbm, bias), (mask_hbm, mask), (ws_hbm, ws), (wn_hbm, wn)))]
    for load in loads:
        load.start()

    def at(way, step):
        return (z + rings - step) % rings if way == 0 else (z + step) % rings

    def zcopy(way, step, piece):
        slot = at(way, step)
        if piece == PIECES:
            src, dst = own if isinstance(step, int) and step == 0 else ringi.at[slot], ringi.at[slot]
        else:
            rows = pl.ds(piece * PIECE, PIECE)
            src = ft_hbm.at[rows] if isinstance(step, int) and step == 0 else ring.at[slot, rows]
            dst = ring.at[slot, rows]
        return pltpu.make_async_remote_copy(
            src_ref=src, dst_ref=dst, send_sem=zs.at[way, step, piece], recv_sem=zr.at[slot, piece],
            device_id=(up if way == 0 else down, x), device_id_type=MESH)

    def zarrived(way, step, piece):
        slot = at(way, step)
        ref = ringi.at[slot] if piece == PIECES else ring.at[slot, pl.ds(piece * PIECE, PIECE)]
        pltpu.make_async_remote_copy(
            src_ref=ref, dst_ref=ref, send_sem=zs.at[way, 0, piece], recv_sem=zr.at[slot, piece],
            device_id=(up, x), device_id_type=MESH).wait_recv()

    order = (PIECES,) + tuple(range(PIECES))
    last = ((PIECES,) + tuple(range(PIECES // 2)), tuple(range(PIECES // 2, PIECES)))

    def forward(step, pieces):
        for piece in pieces:
            for way in (0, 1):
                zarrived(way, step, piece)
                zcopy(way, step, piece).start()

    def ycopy(step, o, rows):
        dest = (me + o) % PLANE
        return pltpu.make_async_remote_copy(
            src_ref=ysend.at[step, dest, pl.ds(0, rows)], dst_ref=yrecv.at[step, me, pl.ds(0, rows)],
            send_sem=ys.at[step, o - 1], recv_sem=yr.at[step, me],
            device_id=(z * PLANE + dest, x), device_id_type=MESH)

    def yarrived(step, rows):
        for o in range(1, PLANE):
            src = (me + o) % PLANE
            pltpu.make_async_remote_copy(
                src_ref=ysend.at[step, src, pl.ds(0, rows)], dst_ref=yrecv.at[step, src, pl.ds(0, rows)],
                send_sem=ys.at[step, o - 1], recv_sem=yr.at[step, src],
                device_id=(z * PLANE + src, x), device_id_type=MESH).wait_recv()

    def fcopy(o):
        return pltpu.make_async_remote_copy(
            src_ref=ft_hbm, dst_ref=xf.at[x], send_sem=fs.at[o - 1], recv_sem=fr.at[x],
            device_id=(dom, (x + o) % feats), device_id_type=MESH)

    def farrived(o):
        src = (x + o) % feats
        pltpu.make_async_remote_copy(
            src_ref=ft_hbm, dst_ref=xf.at[src], send_sem=fs.at[o - 1], recv_sem=fr.at[src],
            device_id=(dom, src), device_id_type=MESH).wait_recv()

    def mcopy(src, part, o, sem):
        rows = pl.ds(384 * part, 384)
        return pltpu.make_async_remote_copy(
            src_ref=xm.at[src, rows], dst_ref=xm.at[src, rows], send_sem=ms.at[sem], recv_sem=mr.at[src, part],
            device_id=(dom, (x + o + feats) % feats), device_id_type=MESH)

    def marrived(o, part):
        mcopy((x + o + feats) % feats, part, 1, 0).wait_recv()

    def select(ref, idref):
        ids = pltpu.roll(idref[0:32, :].astype(F32), (128 - PLANE * z) % 128, 1)
        lane = iota((32, 512), 1).astype(F32) - SHIFT
        pick = [hot(ids[:, d:d + 1] == lane) for d in range(PLANE)]
        edges = idref[32:48, :].astype(F32)
        hub = (iota((32, 128), 0) + z * 32 - SHIFT).astype(F32)
        node = (iota((512, 128), 0) - SHIFT).astype(F32)
        to = jnp.concatenate([hot(hub == edges[4 + c:5 + c, :]) for c in range(4)], axis=1)
        fro = jnp.concatenate([hot(node == edges[c:c + 1, :]) for c in range(4)], axis=1)
        got = dot_nt(jnp.concatenate(pick + [dot_nt(to, fro).astype(BF16)], axis=0), ref[...])
        msum[:, 0:WIDTH] += got[256:288, :]
        return got[0:256, :]

    def widen(tail):
        return jnp.concatenate([tail, jnp.zeros_like(tail)], axis=1)

    low = iota((256, 128), 1) < 64

    def put(step, way, got):
        ysend[step, :, 64 * way:64 * way + 32, :] = got[:, :128].astype(BF16).reshape(PLANE, SLOTS, 128)
        tail = widen(got[:, 128:])
        if way == 1:
            tail = ysend[step, :, 32:64, :].reshape(256, 128).astype(F32) + pltpu.roll(tail, 64, 1)
        ysend[step, :, 32:64, :] = tail.astype(BF16).reshape(PLANE, SLOTS, 128)

    def pick(step, way):
        slot = at(way, step)
        put(step, way, select(ring.at[slot], ringi.at[slot]))

    def send(step, rows):
        for o in (4, 5, 3, 2, 6, 1, 7):
            ycopy(step, o, rows).start()
        yrecv[step, me, 0:rows, :] = ysend[step, me, 0:rows, :]

    def place(step, way, last=False):
        zz = at(way, step)
        to = tgt[pl.ds(zz, 1), :]
        lane = iota((1, 256), 1) % SLOTS
        if last:
            for j in range(4):
                to = jnp.where(lane == 28 + j, hub_local[0:1, j:j + 1].astype(F32), to)
        pos = iota((256, 512), 0)
        slot = pos % SLOTS
        hub = jnp.where((slot >= 24) & (slot < 28), zz * 32 + (pos // SLOTS) * 4 + slot - 24, -1)
        where = dot_nt(hub_hot[...], hot(hub == hub_s[...]))
        where = (where + jnp.where(iota((512, 256), 0).astype(F32) == to, 1.0, 0.0)).astype(BF16)
        rows = jnp.concatenate([yrecv[step, :, 64 * way:64 * way + 32, :].reshape(256, 128),
                                yrecv[step, :, 32:64, :].reshape(256, 128)], axis=1)
        acc = accp if way == 0 else accm
        acc[...] += dot(where, rows)

    def product(i):
        fold = xm[i, 512:768, :]
        carry[0:256, :] += dot(jnp.concatenate([xm[i, 0:256, :], fold], axis=1), wfold[i, 0])
        carry[256:512, :] += dot(jnp.concatenate([xm[i, 256:512, :], fold], axis=1), wfold[i, 1])

    for load in loads[:4]:
        load.wait()
    raw[0:24, :] = (cs[...] - SHIFT).astype(F32)
    row = iota((8, 128), 0)
    hubs = jnp.full((8, 128), 640, I32)
    for j in range(4):
        hubs = jnp.where(row == j, hub_local[0:1, j:j + 1], hubs)
    raw[24:32, :] = (hubs - SHIFT).astype(F32)
    raw[32:36, :] = (mirror_f[...] - SHIFT).astype(F32)
    raw[36:40, :] = (mirror_t[...] - SHIFT).astype(F32)
    raw[40:48, :] = jnp.zeros((8, 128), F32)
    own[...] = raw[...].astype(BF16)

    pl.semaphore_wait(barrier, 2 + PLANE - 1 + feats - 1)
    for piece in order:
        for way in (0, 1):
            zcopy(way, 0, piece).start()
    for o in range(1, feats):
        fcopy(o).start()

    for load in loads[4:]:
        load.wait()
    accp[...] = jnp.zeros_like(accp)
    accm[...] = jnp.zeros_like(accm)
    accl[...] = jnp.zeros_like(accl)
    msum[...] = jnp.zeros_like(msum)

    ysend[0, :, 64:96, :] = jnp.zeros((PLANE, SLOTS, 128), BF16)
    put(0, 0, select(ft, own))
    send(0, 96)

    raw[0:24, :] = ct[...].astype(F32)
    raw[24:48, :] = jnp.full((24, 128), -1.0, F32)
    wide = jnp.transpose(jnp.concatenate([raw[0:32, :], jnp.full((96, 128), -1.0, F32)], axis=0))
    wide = wide[0:rings * PLANE, :].reshape(rings, PLANE, 128)
    lane = iota((rings, 128), 1)
    for part in (0, 1):
        whole = jnp.full((rings, 128), -1.0, F32)
        for d in range(4):
            one = wide[:, 4 * part + d, :]
            whole = jnp.where(lane // SLOTS == d, pltpu.roll(one, SLOTS * d, 1) if d else one, whole)
        tgt[:, 128 * part:128 * part + 128] = whole
    hub_hot[...] = hot(iota((512, 512), 0) == hub_t[...])

    if half > 2:
        forward(1, order)
    else:
        for piece in order:
            for way in (0, 1):
                zarrived(way, 1, piece)
        for way in (0, 1):
            for piece in last[way]:
                zcopy(way, 1, piece).start()

    for t in range(12):
        is_at = [[(tidx[i:i + 1, t:t + 1] == b).astype(F32) for b in range(4)] for i in (0, 1)]
        block = sum(ft[:, 128 * b:128 * b + 128].astype(F32) * is_at[1][b] for b in range(4)).astype(BF16)
        part = dot_nt(mask[t].astype(F32).astype(BF16), block)
        for b in range(4):
            accl[128 * b:128 * b + 128, 0:WIDTH] += part * is_at[0][b]

    for i in range(feats):
        a, b, zero = wn[192 * i:192 * i + 128, :], wn[192 * i + 128:192 * i + 192, :], jnp.zeros((64, 256), BF16)
        wfold[i, 0] = jnp.concatenate([a, b, zero], axis=0)
        wfold[i, 1] = jnp.concatenate([a, zero, b], axis=0)

    def own_columns():
        xf[x] = ft[...]
        for o in range(1, feats):
            farrived(o)
        carry[...] = jnp.zeros_like(carry) + bias[...]

        def one(i, _):
            carry[...] += dot_tn(xf[i], ws[pl.ds(pl.multiple_of(i * WIDTH, 64), WIDTH), :])
            return 0

        lax.fori_loop(0, feats, one, 0)

    def step(k, _):
        forward(k, order[:2])
        pick(k - 1, 0)
        forward(k, order[2:4])
        pick(k - 1, 1)
        forward(k, order[4:5])
        send(k - 1, 96)
        forward(k, order[5:6])
        yarrived(k - 2, 96)
        place(k - 2, 0)
        forward(k, order[6:7])
        place(k - 2, 1)

        @pl.when(k == half // 2)
        def _():
            own_columns()
        return 0

    k = half - 1
    if half > 2:
        lax.fori_loop(2, half - 1, step, 0)
        if half // 2 < 2 or half // 2 >= half - 1:
            own_columns()
        for piece in order:
            for way in (0, 1):
                zarrived(way, k, piece)
                if piece in last[way]:
                    zcopy(way, k, piece).start()
        pick(k - 1, 0)
        pick(k - 1, 1)
        send(k - 1, 96)
    else:
        own_columns()
    pick(k, 0)
    pick(k, 1)
    send(k, 96)
    if half > 2:
        yarrived(k - 2, 96)
        place(k - 2, 0)
        place(k - 2, 1)
    yarrived(k - 1, 96)
    place(k - 1, 0)
    place(k - 1, 1)

    for piece in order:
        zarrived(0, half, piece)
    slot = at(0, half)
    got = select(ring.at[slot], ringi.at[slot])
    row, col = iota((256, 32), 0), iota((256, 32), 1)
    spread = hot((row // SLOTS == col // 4) & (row % SLOTS == 28 + col % 4))
    put(half, 0, got + dot(spread, msum[:, 0:WIDTH].astype(BF16)))
    send(half, 64)
    yarrived(k, 96)
    place(k, 0)
    place(k, 1)
    yarrived(half, 64)
    place(half, 0, last=True)

    degree = deg[...].astype(F32)
    degree = jnp.concatenate([column(degree[i:i + 1, :]) for i in range(4)], axis=0)
    lead = (accp[:, 0:128] + accm[:, 0:128] + accl[:, 0:128]) / degree
    rest = (accp[:, 128:256] + pltpu.roll(accm[:, 128:256], 64, 1) + accl[:, 128:256]) / degree
    xm[x, 0:512, :] = lead.astype(BF16)
    xm[x, 512:768, :] = jnp.where(low, rest[0:256, :], pltpu.roll(rest[256:512, :], 64, 1)).astype(BF16)
    sent = []
    if feats == 4:
        sent = [mcopy(x, 0, 1, 0), mcopy(x, 1, -1, 1), mcopy(x, 1, 1, 2), mcopy(x, 0, -1, 3)]
        for copy in sent:
            copy.start()
        product(x)
        marrived(-1, 0)
        sent.append(mcopy((x + 3) % 4, 0, 1, 4))
        sent[4].start()
        marrived(1, 1)
        sent.append(mcopy((x + 1) % 4, 1, -1, 5))
        sent[5].start()
        marrived(-1, 1)
        product((x + 3) % 4)
        marrived(1, 0)
        product((x + 1) % 4)
        marrived(2, 0)
        marrived(2, 1)
        product((x + 2) % 4)
    else:
        sent = [mcopy(x, part, o, 2 * o + part - 2) for o in range(1, feats) for part in (0, 1)]
        for copy in sent:
            copy.start()
        product(x)
        for o in range(1, feats):
            marrived(o, 0)
            marrived(o, 1)
            product((x + o) % feats)
    out[...] = jnp.maximum(carry[...], 0.0).astype(BF16)

    for way in (0, 1):
        for s in range(half - 1):
            for piece in order:
                zcopy(way, s, piece).wait_send()
        for piece in last[way]:
            zcopy(way, half - 1, piece).wait_send()
    for o in range(1, PLANE):
        for s in range(half):
            ycopy(s, o, 96).wait_send()
        ycopy(half, o, 64).wait_send()
    for o in range(1, feats):
        fcopy(o).wait_send()
    for copy in sent:
        copy.wait_send()


def on_device(rings, feats, features, w_self, w_neigh, out_bias, degrees, tile_index, tile_mask, cut_source, cut_target,
              hub_local, hub_source, hub_target, mirror_source, mirror_target):
    half = rings // 2
    parts = rings * PLANE
    anywhere = pl.BlockSpec(memory_space=pl.ANY)
    args = (features.T, cut_source[0].T, cut_target[0].T, tile_index[0].T, hub_local, hub_target, hub_source,
            mirror_source.reshape(4, 128), mirror_target.reshape(4, 128), degrees.reshape(4, 128), out_bias.reshape(1, 256),
            tile_mask[0], w_self, w_neigh)
    if parts < 128:
        args = args[:1] + tuple(jnp.pad(a, ((0, 0), (0, 128 - parts))) for a in args[1:3]) + args[3:]
    return pl.pallas_call(
        functools.partial(kernel, rings, feats),
        out_shape=jax.ShapeDtypeStruct((512, 256), BF16),
        in_specs=[anywhere] * len(args),
        out_specs=pl.BlockSpec(memory_space=pltpu.VMEM),
        scratch_shapes=[
            pltpu.VMEM((rings, WIDTH, 512), BF16),
            pltpu.VMEM((rings, IDS, 128), BF16),
            pltpu.VMEM((half + 1, PLANE, 96, 128), BF16),
            pltpu.VMEM((half + 1, PLANE, 96, 128), BF16),
            pltpu.VMEM((feats, WIDTH, 512), BF16),
            pltpu.VMEM((feats, 768, 128), BF16),
            pltpu.VMEM((512, 256), F32),
            pltpu.VMEM((512, 256), F32),
            pltpu.VMEM((512, 256), F32),
            pltpu.VMEM((32, 256), F32),
            pltpu.VMEM((512, 512), BF16),
            pltpu.VMEM((feats, 2, 256, 256), BF16),
            pltpu.VMEM((512, 256), F32),
            pltpu.VMEM((IDS, 128), BF16),
            pltpu.VMEM((rings, 256), F32),
            pltpu.VMEM((IDS, 128), F32),
        ] + [pltpu.VMEM(a.shape, a.dtype) for a in args] + [
            pltpu.SemaphoreType.DMA((2, half, PIECES + 1)),
            pltpu.SemaphoreType.DMA((rings, PIECES + 1)),
            pltpu.SemaphoreType.DMA((half + 1, PLANE)),
            pltpu.SemaphoreType.DMA((half + 1, PLANE)),
            pltpu.SemaphoreType.DMA((4,)),
            pltpu.SemaphoreType.DMA((4,)),
            pltpu.SemaphoreType.DMA((6,)),
            pltpu.SemaphoreType.DMA((4, 2)),
            pltpu.SemaphoreType.DMA((len(args),)),
        ],
        compiler_params=pltpu.CompilerParams(
            collective_id=0, has_side_effects=True, vmem_limit_bytes=40 * 1024 * 1024),
        cost_estimate=pl.CostEstimate(flops=10**10, bytes_accessed=4 * 10**6, transcendentals=0),
    )(*args)


def solution(mesh):
    return jax.shard_map(
        functools.partial(on_device, mesh.shape["dom"] // PLANE, mesh.shape["feat"]),
        mesh=mesh,
        in_specs=(P("dom", "feat"), P(None, "feat"), P(None, "feat"), P("feat"), P("dom"), P("dom"), P("dom"), P("dom"),
                  P("dom"), P("dom"), P("dom"), P("dom"), P("dom"), P("dom")),
        out_specs=P("dom", "feat"),
        check_vma=False,
    )
```

time: 147 us -> 81.2 us (0.55)
  waiting for transfers between devices: 78.1 us -> 0 us
  Pallas kernels: 0 us -> 71 us
  blocking collectives: 27.3 us -> 0 us
  starting transfers between devices: 20.6 us -> 0 us
  matrix products: 13.2 us -> 0 us
  local copies, waits for them, and re-layouts: 4.14 us -> 9.55 us
  other arithmetic: 3.01 us -> 0 us
    all_to_all x1 -> x0, waiting for transfers between devices: 78.1 us -> none  [on_device(): lax.all_to_all(message, 'dom', split_axis=0, concat_axis=0, tiled=True)]
    pallas_call x0 -> x1, Pallas kernels: none -> 71 us  [on_device(): pl.pallas_call(functools.partial(kernel, rings, feats), out_shape=jax.Sha...]
    all_gather x2 -> x0, blocking collectives: 27.3 us -> none  [the longest x1 13.9 us: on_device(): all_features = lax.all_gather(features, 'feat', axis=1, tiled=True)]
    all_to_all x1 -> x0, starting transfers between devices: 20.6 us -> none  [on_device(): lax.all_to_all(message, 'dom', split_axis=0, concat_axis=0, tiled=True)]
    dot_general x9 -> x0, matrix products: 13.2 us -> none  [the longest x8 12.8 us: on_device(): dot = lambda a, b: jnp.dot(a, b, preferred_element_type=f32)]
    unnamed x33 -> x29, local copies, waits for them, and re-layouts: 0.19 us -> 9.55 us
    concatenate x1 -> x0, other arithmetic: 2.09 us -> none  [on_device(): jnp.concatenate([outgoing, jnp.broadcast_to(own_hubs[None], (parts, hub_d...]
    convert_element_type x3 -> x0, local copies, waits for them, and re-layouts: 2.05 us -> none  [the longest x1 1.24 us: on_device(): adjacency.astype(bf16)]
  transfers between devices with their start and end apart: 1 -> 0, of which waited for: 1 -> 0; matrix products, arithmetic and copies ran while one was open for 4% -> 0% of each run, Pallas kernels for 0% -> 0%
where the time goes in v3:
time: 81.2 us; the launch traced here: 80.6 us
  Pallas kernels  71 us (87%)
  local copies, waits for them, and re-layouts  9.55 us (12%)
    pallas_call x1, Pallas kernels, on_device(): pl.pallas_call(functools.partial(kernel, rings, feats), out_shape=jax.Sha...  71 us
    unnamed x29, local copies, waits for them, and re-layouts  9.55 us

profile of v3, /device:TPU:6, one launch (start us, length us, event | category | flops | bytes accessed | tf_op | source)
XLA Modules:
  0.0 80.6 jit_solution(15658571857616185433)
XLA Ops:
  0.0 0.0 copy-start.4
  0.0 0.0 copy-start.7
  0.0 0.0 copy-start.6
  0.0 0.0 copy-start.11
  0.0 0.7 copy-done.4
  0.7 0.0 copy-done.7
  0.7 0.0 copy-done.6
  0.7 0.0 copy-done.11
  0.7 0.0 copy-start
  0.7 1.1 %copy-done = s32[1,12,128,128]{3,2,1,0:T(8,128)S(1)} copy-done((s32[1,12,128,128]{3,2,1,0:T(8,128)S(1)}, s32[1,12,128,128]{3,2,1,0:T(8,128)}, u32[]{:S(2)}) %copy-start) | copy-done | bytes 786456
  1.9 0.0 copy-start.1
  1.9 1.0 %copy-done.1 = bf16[768,256]{1,0:T(8,128)(2,1)S(1)} copy-done((bf16[768,256]{1,0:T(8,128)(2,1)S(1)}, bf16[768,256]{1,0:T(8,128)(2,1)}, u32[]{:S(2)}) %copy-start.1) | copy-done | bytes 393240
  2.9 0.0 copy-start.2
  2.9 1.0 %copy-done.2 = bf16[768,256]{1,0:T(8,128)(2,1)S(1)} copy-done((bf16[768,256]{1,0:T(8,128)(2,1)S(1)}, bf16[768,256]{1,0:T(8,128)(2,1)}, u32[]{:S(2)}) %copy-start.2) | copy-done | bytes 393240
  3.9 0.0 copy-start.3
  3.9 0.9 %copy-done.3 = bf16[512,192]{0,1:T(8,128)(2,1)S(1)} copy-done((bf16[512,192]{0,1:T(8,128)(2,1)S(1)}, bf16[512,192]{0,1:T(8,128)(2,1)}, u32[]{:S(2)}) %copy-start.3) | copy-done | bytes 196632
  4.8 0.0 copy-start.5
  4.8 0.7 copy-done.5
  5.5 0.0 copy-start.8
  5.5 0.7 copy-done.8
  6.2 0.0 copy-start.9
  6.2 0.7 copy-done.9
  6.9 0.0 copy-start.10
  6.9 0.7 copy-done.10
  7.5 0.0 copy-start.12
  7.5 0.7 copy-done.12
  8.2 0.0 copy-start.13
  8.2 0.7 copy-done.13
  8.9 71.0 %shard_map.136 = bf16[512,256]{1,0:T(8,128)(2,1)S(1)} custom-call(bf16[192,512]{1,0:T(8,128)(2,1)S(1)} %bitcast.16, s32[24,128]{1,0:T(8,128)S(1)} %bitcast.17, s32[24,128]{1,0:T(8,128)S(1)} %bitcast.18, s32[2,12]{1,0:T(2,128)S(1)} %bitcast.22, s32[1,4]{1,0:T(1,128)S(1)} %copy-done.13, s32[1,512]{1,0:T(1,128)S(1)} %copy-done.6, s32[1,512]{1,0:T(1,128)S(1)} %copy-done.7, ...), custom_call_target="tpu_custom_call" | custom-call | flops 10000000000 | bytes 4000000 | tf_op jit(solution)/shard_map/pallas_call | solution.py:387
  79.9 0.7 copy.16
Async XLA Ops:
  0.0 0.7 copy-start.4
  0.0 0.7 copy-start.7
  0.0 0.7 copy-start.6
  0.0 0.7 copy-start.11
  0.7 1.1 %copy-start = (s32[1,12,128,128]{3,2,1,0:T(8,128)S(1)}, s32[1,12,128,128]{3,2,1,0:T(8,128)}, u32[]{:S(2)}) copy-start(s32[1,12,128,128]{3,2,1,0:T(8,128)} %param.20) | copy-start | bytes 2359300
  1.9 1.0 %copy-start.1 = (bf16[768,256]{1,0:T(8,128)(2,1)S(1)}, bf16[768,256]{1,0:T(8,128)(2,1)}, u32[]{:S(2)}) copy-start(bf16[768,256]{1,0:T(8,128)(2,1)} %ws_hbm.1) | copy-start | bytes 1179652
  2.9 1.0 %copy-start.2 = (bf16[768,256]{1,0:T(8,128)(2,1)S(1)}, bf16[768,256]{1,0:T(8,128)(2,1)}, u32[]{:S(2)}) copy-start(bf16[768,256]{1,0:T(8,128)(2,1)} %wn_hbm.1) | copy-start | bytes 1179652
  3.9 0.9 %copy-start.3 = (bf16[512,192]{0,1:T(8,128)(2,1)S(1)}, bf16[512,192]{0,1:T(8,128)(2,1)}, u32[]{:S(2)}) copy-start(bf16[512,192]{0,1:T(8,128)(2,1)} %param.14) | copy-start | bytes 589828
  4.8 0.7 copy-start.5
  5.5 0.7 copy-start.8
  6.2 0.7 copy-start.9
  6.9 0.7 copy-start.10
  7.5 0.7 copy-start.12
  8.2 0.7 copy-start.13

commit v4 on v3

--- a/solution.py
+++ b/solution.py
@@ -14,6 +14,7 @@
 WIDTH = 192
 PIECES, PIECE = 6, 32
 IDS = 48
+DIRECT = 2
 SHIFT = 256
 
 
@@ -42,19 +43,26 @@
 
 
 def kernel(rings, feats, ft_hbm, cs_hbm, ct_hbm, ti_hbm, hl_hbm, ht_hbm, hs_hbm, mf_hbm, mt_hbm, deg_hbm, bias_hbm,
-           mask_hbm, ws_hbm, wn_hbm, out, ring, ringi, ysend, yrecv, xf, xm, accp, accm, accl, msum, hub_hot, wfold, carry,
+           mask_hbm, ws_hbm, wn_hbm, out, ring, ringi, ysend, yrecv, lsend, lrecv, xf, xm, accp, accm, accl, msum, hub_hot, wfold, carry,
            own, tgt, raw, ft, cs, ct, tidx, hub_local, hub_t, hub_s, mirror_f, mirror_t, deg, bias, mask, ws, wn,
-           zs, zr, ys, yr, fs, fr, ms, mr, local):
+           zs, zr, ys, yr, ls, lr, fs, fr, ms, mr, local):
     half = rings // 2
+    reach = half - DIRECT
     dom, x = lax.axis_index("dom"), lax.axis_index("feat")
     z, me = dom // PLANE, dom % PLANE
     up, down = ((z + 1) % rings) * PLANE + me, ((z + rings - 1) % rings) * PLANE + me
 
     barrier = pltpu.get_barrier_semaphore()
-    for dev in (up, down):
-        pl.semaphore_signal(barrier, inc=1, device_id=(dev, x), device_id_type=MESH)
-    for o in range(1, PLANE):
-        pl.semaphore_signal(barrier, inc=1, device_id=(z * PLANE + (me + o) % PLANE, x), device_id_type=MESH)
+    def greet(plane, dest):
+        pl.semaphore_signal(barrier, inc=1, device_id=(plane * PLANE + dest, x), device_id_type=MESH)
+
+    for o in range(PLANE):
+        if o:
+            greet(z, (me + o) % PLANE)
+        if DIRECT > 1:
+            greet((z + 1) % rings, (me + o) % PLANE)
+            greet((z + rings - 1) % rings, (me + o) % PLANE)
+        greet((z + rings - DIRECT + 2 * DIRECT * (me // 4)) % rings, (me + o) % PLANE)
     for o in range(1, feats):
         pl.semaphore_signal(barrier, inc=1, device_id=(dom, (x + o) % feats), device_id_type=MESH)
 
@@ -87,7 +95,6 @@
             device_id=(up, x), device_id_type=MESH).wait_recv()
 
     order = (PIECES,) + tuple(range(PIECES))
-    last = ((PIECES,) + tuple(range(PIECES // 2)), tuple(range(PIECES // 2, PIECES)))
 
     def forward(step, pieces):
         for piece in pieces:
@@ -110,6 +117,26 @@
                 send_sem=ys.at[step, o - 1], recv_sem=yr.at[step, src],
                 device_id=(z * PLANE + src, x), device_id_type=MESH).wait_recv()
 
+    kinds = [(d, way) for d in range(reach + 1, half) for way in (0, 1)] + [(half, 0)]
+
+    def beyond(way):
+        wants = []
+        for d in range(reach + 1, half + 1):
+            plane = (z + d - reach) % rings if way == 0 else (z + rings - d + reach) % rings
+            wants.append((kinds.index((d, way)), plane, 0, 8) if d < half else (len(kinds) - 1, plane, 4 * way, 4))
+        return wants
+
+    def lcopy(kind, plane, dest):
+        return pltpu.make_async_remote_copy(
+            src_ref=lsend.at[kind, dest], dst_ref=lrecv.at[kind, me], send_sem=ls.at[kind, dest], recv_sem=lr.at[kind, me],
+            device_id=(plane * PLANE + dest, x), device_id_type=MESH)
+
+    def larrived(kind):
+        for src in range(PLANE):
+            pltpu.make_async_remote_copy(
+                src_ref=lsend.at[kind, src], dst_ref=lrecv.at[kind, src], send_sem=ls.at[kind, src], recv_sem=lr.at[kind, src],
+                device_id=(up, x), device_id_type=MESH).wait_recv()
+
     def fcopy(o):
         return pltpu.make_async_remote_copy(
             src_ref=ft_hbm, dst_ref=xf.at[x], send_sem=fs.at[o - 1], recv_sem=fr.at[x],
@@ -130,18 +157,31 @@
     def marrived(o, part):
         mcopy((x + o + feats) % feats, part, 1, 0).wait_recv()
 
-    def select(ref, idref):
-        ids = pltpu.roll(idref[0:32, :].astype(F32), (128 - PLANE * z) % 128, 1)
+    def select(ref, idref, wants):
+        ids = idref[0:32, :].astype(F32)
         lane = iota((32, 512), 1).astype(F32) - SHIFT
-        pick = [hot(ids[:, d:d + 1] == lane) for d in range(PLANE)]
         edges = idref[32:48, :].astype(F32)
-        hub = (iota((32, 128), 0) + z * 32 - SHIFT).astype(F32)
         node = (iota((512, 128), 0) - SHIFT).astype(F32)
-        to = jnp.concatenate([hot(hub == edges[4 + c:5 + c, :]) for c in range(4)], axis=1)
         fro = jnp.concatenate([hot(node == edges[c:c + 1, :]) for c in range(4)], axis=1)
-        got = dot_nt(jnp.concatenate(pick + [dot_nt(to, fro).astype(BF16)], axis=0), ref[...])
-        msum[:, 0:WIDTH] += got[256:288, :]
-        return got[0:256, :]
+        picks, tos = [], []
+        for plane, first, count in wants:
+            here = pltpu.roll(ids, (128 - PLANE * plane) % 128, 1)
+            picks += [hot(here[:, d:d + 1] == lane) for d in range(first, first + count)]
+            hub = (iota((4 * count, 128), 0) + plane * 32 + 4 * first - SHIFT).astype(F32)
+            tos.append(jnp.concatenate([hot(hub == edges[4 + c:5 + c, :]) for c in range(4)], axis=1))
+        counts = dot_nt(jnp.concatenate(tos, axis=0), fro).astype(BF16)
+        got = dot_nt(jnp.concatenate(picks + [counts], axis=0), ref[...])
+        total = SLOTS * len(picks)
+        out, at_row, at_sum = [], 0, total
+        for _, _, count in wants:
+            out.append((got[at_row:at_row + SLOTS * count, :], got[at_sum:at_sum + 4 * count, :]))
+            at_row, at_sum = at_row + SLOTS * count, at_sum + 4 * count
+        return out
+
+    def spread(sums):
+        count = sums.shape[0] // 4
+        row, col = iota((SLOTS * count, 4 * count), 0), iota((SLOTS * count, 4 * count), 1)
+        return dot(hot((row // SLOTS == col // 4) & (row % SLOTS == 28 + col % 4)), sums.astype(BF16))
 
     def widen(tail):
         return jnp.concatenate([tail, jnp.zeros_like(tail)], axis=1)
@@ -157,18 +197,33 @@
 
     def pick(step, way):
         slot = at(way, step)
-        put(step, way, select(ring.at[slot], ringi.at[slot]))
+        (got, sums), = select(ring.at[slot], ringi.at[slot], [(z, 0, PLANE)])
+        msum[:, 0:WIDTH] += sums
+        put(step, way, got)
+
+    def pick_beyond(way):
+        slot, wants = at(way, reach), beyond(way)
+        got = select(ring.at[slot], ringi.at[slot], [want[1:] for want in wants] + [(z, 0, PLANE)])
+        for (kind, plane, first, count), (rows, sums) in zip(wants, got):
+            rows = rows + spread(sums)
+            lsend[kind, first:first + count, 0:32, :] = rows[:, 0:128].astype(BF16).reshape(count, SLOTS, 128)
+            tail = widen(rows[:, 128:]).reshape(count, 2, 16, 128)
+            tail = tail[:, 0].reshape(16 * count, 128) + pltpu.roll(tail[:, 1].reshape(16 * count, 128), 64, 1)
+            lsend[kind, first:first + count, 32:48, :] = tail.astype(BF16).reshape(count, 16, 128)
+            for o in range(count):
+                lcopy(kind, plane, first + (me + o) % count).start()
+        msum[:, 0:WIDTH] += got[-1][1]
+        return got[-1][0]
 
     def send(step, rows):
         for o in (4, 5, 3, 2, 6, 1, 7):
             ycopy(step, o, rows).start()
         yrecv[step, me, 0:rows, :] = ysend[step, me, 0:rows, :]
 
-    def place(step, way, last=False):
-        zz = at(way, step)
+    def place(zz, rows, way, sums=False):
         to = tgt[pl.ds(zz, 1), :]
         lane = iota((1, 256), 1) % SLOTS
-        if last:
+        if sums:
             for j in range(4):
                 to = jnp.where(lane == 28 + j, hub_local[0:1, j:j + 1].astype(F32), to)
         pos = iota((256, 512), 0)
@@ -176,10 +231,18 @@
         hub = jnp.where((slot >= 24) & (slot < 28), zz * 32 + (pos // SLOTS) * 4 + slot - 24, -1)
         where = dot_nt(hub_hot[...], hot(hub == hub_s[...]))
         where = (where + jnp.where(iota((512, 256), 0).astype(F32) == to, 1.0, 0.0)).astype(BF16)
-        rows = jnp.concatenate([yrecv[step, :, 64 * way:64 * way + 32, :].reshape(256, 128),
-                                yrecv[step, :, 32:64, :].reshape(256, 128)], axis=1)
         acc = accp if way == 0 else accm
         acc[...] += dot(where, rows)
+
+    def place_near(step, way, sums=False):
+        place(at(way, step), jnp.concatenate([yrecv[step, :, 64 * way:64 * way + 32, :].reshape(256, 128),
+                                              yrecv[step, :, 32:64, :].reshape(256, 128)], axis=1), way, sums)
+
+    def place_late(kind):
+        tail = lrecv[kind, :, 32:48, :].astype(F32).reshape(128, 128)
+        tail = jnp.concatenate([tail.reshape(PLANE, 1, 16, 128), pltpu.roll(tail, 64, 1).reshape(PLANE, 1, 16, 128)], axis=1)
+        rows = jnp.concatenate([lrecv[kind, :, 0:32, :].reshape(256, 128), tail.astype(BF16).reshape(256, 128)], axis=1)
+        place(at(kinds[kind][1], kinds[kind][0]), rows, 0, True)
 
     def product(i):
         fold = xm[i, 512:768, :]
@@ -199,7 +262,7 @@
     raw[40:48, :] = jnp.zeros((8, 128), F32)
     own[...] = raw[...].astype(BF16)
 
-    pl.semaphore_wait(barrier, 2 + PLANE - 1 + feats - 1)
+    pl.semaphore_wait(barrier, PLANE * (2 * DIRECT) - 1 + feats - 1)
     for piece in order:
         for way in (0, 1):
             zcopy(way, 0, piece).start()
@@ -214,7 +277,9 @@
     msum[...] = jnp.zeros_like(msum)
 
     ysend[0, :, 64:96, :] = jnp.zeros((PLANE, SLOTS, 128), BF16)
-    put(0, 0, select(ft, own))
+    (got, sums), = select(ft, own, [(z, 0, PLANE)])
+    msum[:, 0:WIDTH] += sums
+    put(0, 0, got)
     send(0, 96)
 
     raw[0:24, :] = ct[...].astype(F32)
@@ -230,22 +295,14 @@
         tgt[:, 128 * part:128 * part + 128] = whole
     hub_hot[...] = hot(iota((512, 512), 0) == hub_t[...])
 
-    if half > 2:
-        forward(1, order)
-    else:
-        for piece in order:
-            for way in (0, 1):
-                zarrived(way, 1, piece)
-        for way in (0, 1):
-            for piece in last[way]:
-                zcopy(way, 1, piece).start()
-
     for t in range(12):
         is_at = [[(tidx[i:i + 1, t:t + 1] == b).astype(F32) for b in range(4)] for i in (0, 1)]
         block = sum(ft[:, 128 * b:128 * b + 128].astype(F32) * is_at[1][b] for b in range(4)).astype(BF16)
         part = dot_nt(mask[t].astype(F32).astype(BF16), block)
         for b in range(4):
             accl[128 * b:128 * b + 128, 0:WIDTH] += part * is_at[0][b]
+
+    forward(1, order)
 
     for i in range(feats):
         a, b, zero = wn[192 * i:192 * i + 128, :], wn[192 * i + 128:192 * i + 192, :], jnp.zeros((64, 256), BF16)
@@ -273,54 +330,44 @@
         send(k - 1, 96)
         forward(k, order[5:6])
         yarrived(k - 2, 96)
-        place(k - 2, 0)
+        place_near(k - 2, 0)
         forward(k, order[6:7])
-        place(k - 2, 1)
+        place_near(k - 2, 1)
 
         @pl.when(k == half // 2)
         def _():
             own_columns()
         return 0
 
-    k = half - 1
-    if half > 2:
-        lax.fori_loop(2, half - 1, step, 0)
-        if half // 2 < 2 or half // 2 >= half - 1:
-            own_columns()
-        for piece in order:
-            for way in (0, 1):
-                zarrived(way, k, piece)
-                if piece in last[way]:
-                    zcopy(way, k, piece).start()
-        pick(k - 1, 0)
-        pick(k - 1, 1)
-        send(k - 1, 96)
-    else:
+    lax.fori_loop(2, reach, step, 0)
+    if not 2 <= half // 2 < reach:
         own_columns()
-    pick(k, 0)
-    pick(k, 1)
+
+    k = reach
+    pick(k - 1, 0)
+    pick(k - 1, 1)
+    send(k - 1, 96)
+    yarrived(k - 2, 96)
+    place_near(k - 2, 0)
+    place_near(k - 2, 1)
+    for piece in order:
+        zarrived(0, k, piece)
+    up_rows = pick_beyond(0)
+    for piece in order:
+        zarrived(1, k, piece)
+    down_rows = pick_beyond(1)
+    put(k, 0, up_rows + spread(msum[:, 0:WIDTH]))
+    put(k, 1, down_rows)
     send(k, 96)
-    if half > 2:
-        yarrived(k - 2, 96)
-        place(k - 2, 0)
-        place(k - 2, 1)
     yarrived(k - 1, 96)
-    place(k - 1, 0)
-    place(k - 1, 1)
-
-    for piece in order:
-        zarrived(0, half, piece)
-    slot = at(0, half)
-    got = select(ring.at[slot], ringi.at[slot])
-    row, col = iota((256, 32), 0), iota((256, 32), 1)
-    spread = hot((row // SLOTS == col // 4) & (row % SLOTS == 28 + col % 4))
-    put(half, 0, got + dot(spread, msum[:, 0:WIDTH].astype(BF16)))
-    send(half, 64)
+    place_near(k - 1, 0)
+    place_near(k - 1, 1)
     yarrived(k, 96)
-    place(k, 0)
-    place(k, 1)
-    yarrived(half, 64)
-    place(half, 0, last=True)
+    place_near(k, 0, True)
+    place_near(k, 1)
+    for kind in range(len(kinds)):
+        larrived(kind)
+        place_late(kind)
 
     degree = deg[...].astype(F32)
     degree = jnp.concatenate([column(degree[i:i + 1, :]) for i in range(4)], axis=0)
@@ -359,15 +406,15 @@
     out[...] = jnp.maximum(carry[...], 0.0).astype(BF16)
 
     for way in (0, 1):
-        for s in range(half - 1):
+        for s in range(reach):
             for piece in order:
                 zcopy(way, s, piece).wait_send()
-        for piece in last[way]:
-            zcopy(way, half - 1, piece).wait_send()
+        for kind, plane, first, count in beyond(way):
+            for dest in range(first, first + count):
+                lcopy(kind, plane, dest).wait_send()
     for o in range(1, PLANE):
-        for s in range(half):
+        for s in range(reach + 1):
             ycopy(s, o, 96).wait_send()
-        ycopy(half, o, 64).wait_send()
     for o in range(1, feats):
         fcopy(o).wait_send()
     for copy in sent:
@@ -377,6 +424,7 @@
 def on_device(rings, feats, features, w_self, w_neigh, out_bias, degrees, tile_index, tile_mask, cut_source, cut_target,
               hub_local, hub_source, hub_target, mirror_source, mirror_target):
     half = rings // 2
+    reach = half - DIRECT
     parts = rings * PLANE
     anywhere = pl.BlockSpec(memory_space=pl.ANY)
     args = (features.T, cut_source[0].T, cut_target[0].T, tile_index[0].T, hub_local, hub_target, hub_source,
@@ -392,8 +440,10 @@
         scratch_shapes=[
             pltpu.VMEM((rings, WIDTH, 512), BF16),
             pltpu.VMEM((rings, IDS, 128), BF16),
-            pltpu.VMEM((half + 1, PLANE, 96, 128), BF16),
-            pltpu.VMEM((half + 1, PLANE, 96, 128), BF16),
+            pltpu.VMEM((reach + 1, PLANE, 96, 128), BF16),
+            pltpu.VMEM((reach + 1, PLANE, 96, 128), BF16),
+            pltpu.VMEM((2 * DIRECT - 1, PLANE, 48, 128), BF16),
+            pltpu.VMEM((2 * DIRECT - 1, PLANE, 48, 128), BF16),
             pltpu.VMEM((feats, WIDTH, 512), BF16),
             pltpu.VMEM((feats, 768, 128), BF16),
             pltpu.VMEM((512, 256), F32),
@@ -407,10 +457,12 @@
             pltpu.VMEM((rings, 256), F32),
             pltpu.VMEM((IDS, 128), F32),
         ] + [pltpu.VMEM(a.shape, a.dtype) for a in args] + [
-            pltpu.SemaphoreType.DMA((2, half, PIECES + 1)),
+            pltpu.SemaphoreType.DMA((2, reach, PIECES + 1)),
             pltpu.SemaphoreType.DMA((rings, PIECES + 1)),
-            pltpu.SemaphoreType.DMA((half + 1, PLANE)),
-            pltpu.SemaphoreType.DMA((half + 1, PLANE)),
+            pltpu.SemaphoreType.DMA((reach + 1, PLANE)),
+            pltpu.SemaphoreType.DMA((reach + 1, PLANE)),
+            pltpu.SemaphoreType.DMA((2 * DIRECT - 1, PLANE)),
+            pltpu.SemaphoreType.DMA((2 * DIRECT - 1, PLANE)),
             pltpu.SemaphoreType.DMA((4,)),
             pltpu.SemaphoreType.DMA((4,)),
             pltpu.SemaphoreType.DMA((6,)),
@@ -418,7 +470,7 @@
             pltpu.SemaphoreType.DMA((len(args),)),
         ],
         compiler_params=pltpu.CompilerParams(
-            collective_id=0, has_side_effects=True, vmem_limit_bytes=40 * 1024 * 1024),
+            collective_id=0, has_side_effects=True, vmem_limit_bytes=60 * 1024 * 1024),
         cost_estimate=pl.CostEstimate(flops=10**10, bytes_accessed=4 * 10**6, transcendentals=0),
     )(*args)
 

time: 81.2 us -> 70.7 us (0.87)
  local copies, waits for them, and re-layouts: 9.55 us -> 1.67 us
  Pallas kernels: 71 us -> 68.7 us
    unnamed x29 -> x1, local copies, waits for them, and re-layouts: 9.55 us -> 1.67 us
    pallas_call x1, Pallas kernels: 71 us -> 68.7 us  [on_device(): pl.pallas_call(functools.partial(kernel, rings, feats), out_shape=jax.Sha...]
where the time goes in v4:
time: 70.7 us; the launch traced here: 70.3 us
  Pallas kernels  68.7 us (97%)
  local copies, waits for them, and re-layouts  1.67 us (2%)
    pallas_call x1, Pallas kernels, on_device(): pl.pallas_call(functools.partial(kernel, rings, feats), out_shape=jax.Sha...  68.7 us
    unnamed x1, local copies, waits for them, and re-layouts  1.67 us

profile of v4, /device:TPU:6, one launch (start us, length us, event | category | flops | bytes accessed | tf_op | source)
XLA Modules:
  0.0 70.3 jit_solution(14519894516700502312)
XLA Ops:
  0.0 68.7 %shard_map.136 = bf16[512,256]{1,0:T(8,128)(2,1)} custom-call(bf16[192,512]{1,0:T(8,128)(2,1)} %bitcast.16, s32[24,128]{1,0:T(8,128)} %bitcast.17, s32[24,128]{1,0:T(8,128)} %bitcast.18, s32[2,12]{1,0:T(2,128)} %bitcast.22, s32[1,4]{1,0:T(1,128)} %hl_hbm.1, s32[1,512]{1,0:T(1,128)} %ht_hbm.1, s32[1,512]{1,0:T(1,128)} %hs_hbm.1, s32[4,128]{1,0:T(4,128)} %bitcast.19, ...), custom_call_target="tpu_custom_call" | custom-call | flops 10000000000 | bytes 4000000 | tf_op jit(solution)/shard_map/pallas_call | solution.py:435
  68.7 1.7 %copy.16 = bf16[512,256]{1,0:T(8,128)(2,1)} copy(bf16[512,256]{1,0:T(8,128)(2,1)} %shard_map.136) | data formatting | bytes 524288

commit v5 on v4

--- a/solution.py
+++ b/solution.py
@@ -43,7 +43,7 @@
 
 
 def kernel(rings, feats, ft_hbm, cs_hbm, ct_hbm, ti_hbm, hl_hbm, ht_hbm, hs_hbm, mf_hbm, mt_hbm, deg_hbm, bias_hbm,
-           mask_hbm, ws_hbm, wn_hbm, out, ring, ringi, ysend, yrecv, lsend, lrecv, xf, xm, accp, accm, accl, msum, hub_hot, wfold, carry,
+           mask_hbm, ws_hbm, wn_hbm, out, ring, ringi, ysend, yrecv, lsend, lrecv, xf, xm, accp, accm, accl, msum, hub_hot, farsel, places, degree, carry,
            own, tgt, raw, ft, cs, ct, tidx, hub_local, hub_t, hub_s, mirror_f, mirror_t, deg, bias, mask, ws, wn,
            zs, zr, ys, yr, ls, lr, fs, fr, ms, mr, local):
     half = rings // 2
@@ -102,19 +102,19 @@
                 zarrived(way, step, piece)
                 zcopy(way, step, piece).start()
 
-    def ycopy(step, o, rows):
+    def ycopy(step, o, first, rows, sem):
         dest = (me + o) % PLANE
         return pltpu.make_async_remote_copy(
-            src_ref=ysend.at[step, dest, pl.ds(0, rows)], dst_ref=yrecv.at[step, me, pl.ds(0, rows)],
-            send_sem=ys.at[step, o - 1], recv_sem=yr.at[step, me],
+            src_ref=ysend.at[step, dest, pl.ds(first, rows)], dst_ref=yrecv.at[step, me, pl.ds(first, rows)],
+            send_sem=ys.at[sem, o - 1], recv_sem=yr.at[sem, me],
             device_id=(z * PLANE + dest, x), device_id_type=MESH)
 
-    def yarrived(step, rows):
+    def yarrived(step, first=0, rows=96, sem=None):
         for o in range(1, PLANE):
             src = (me + o) % PLANE
+            ref = yrecv.at[step, src, pl.ds(first, rows)]
             pltpu.make_async_remote_copy(
-                src_ref=ysend.at[step, src, pl.ds(0, rows)], dst_ref=yrecv.at[step, src, pl.ds(0, rows)],
-                send_sem=ys.at[step, o - 1], recv_sem=yr.at[step, src],
+                src_ref=ref, dst_ref=ref, send_sem=ys.at[step, o - 1], recv_sem=yr.at[step if sem is None else sem, src],
                 device_id=(z * PLANE + src, x), device_id_type=MESH).wait_recv()
 
     kinds = [(d, way) for d in range(reach + 1, half) for way in (0, 1)] + [(half, 0)]
@@ -126,16 +126,21 @@
             wants.append((kinds.index((d, way)), plane, 0, 8) if d < half else (len(kinds) - 1, plane, 4 * way, 4))
         return wants
 
-    def lcopy(kind, plane, dest):
+    late = (pl.ds(0, 32), pl.ds(32, 16))
+
+    def lcopy(kind, plane, dest, part):
         return pltpu.make_async_remote_copy(
-            src_ref=lsend.at[kind, dest], dst_ref=lrecv.at[kind, me], send_sem=ls.at[kind, dest], recv_sem=lr.at[kind, me],
+            src_ref=lsend.at[kind, dest, late[part]], dst_ref=lrecv.at[kind, me, late[part]],
+            send_sem=ls.at[kind, dest, part], recv_sem=lr.at[kind, me, part],
             device_id=(plane * PLANE + dest, x), device_id_type=MESH)
 
-    def larrived(kind):
-        for src in range(PLANE):
-            pltpu.make_async_remote_copy(
-                src_ref=lsend.at[kind, src], dst_ref=lrecv.at[kind, src], send_sem=ls.at[kind, src], recv_sem=lr.at[kind, src],
-                device_id=(up, x), device_id_type=MESH).wait_recv()
+    def larrived(part):
+        for kind in range(len(kinds)):
+            for src in range(PLANE):
+                ref = lrecv.at[kind, src, late[part]]
+                pltpu.make_async_remote_copy(
+                    src_ref=ref, dst_ref=ref, send_sem=ls.at[kind, src, part], recv_sem=lr.at[kind, src, part],
+                    device_id=(up, x), device_id_type=MESH).wait_recv()
 
     def fcopy(o):
         return pltpu.make_async_remote_copy(
@@ -148,16 +153,17 @@
             src_ref=ft_hbm, dst_ref=xf.at[src], send_sem=fs.at[o - 1], recv_sem=fr.at[src],
             device_id=(dom, src), device_id_type=MESH).wait_recv()
 
+    parts = (pl.ds(0, 256), pl.ds(256, 256), pl.ds(512, 128), pl.ds(640, 128))
+
     def mcopy(src, part, o, sem):
-        rows = pl.ds(384 * part, 384)
         return pltpu.make_async_remote_copy(
-            src_ref=xm.at[src, rows], dst_ref=xm.at[src, rows], send_sem=ms.at[sem], recv_sem=mr.at[src, part],
+            src_ref=xm.at[src, parts[part]], dst_ref=xm.at[src, parts[part]], send_sem=ms.at[sem], recv_sem=mr.at[src, part],
             device_id=(dom, (x + o + feats) % feats), device_id_type=MESH)
 
     def marrived(o, part):
         mcopy((x + o + feats) % feats, part, 1, 0).wait_recv()
 
-    def select(ref, idref, wants):
+    def selector(idref, wants):
         ids = idref[0:32, :].astype(F32)
         lane = iota((32, 512), 1).astype(F32) - SHIFT
         edges = idref[32:48, :].astype(F32)
@@ -169,14 +175,12 @@
             picks += [hot(here[:, d:d + 1] == lane) for d in range(first, first + count)]
             hub = (iota((4 * count, 128), 0) + plane * 32 + 4 * first - SHIFT).astype(F32)
             tos.append(jnp.concatenate([hot(hub == edges[4 + c:5 + c, :]) for c in range(4)], axis=1))
-        counts = dot_nt(jnp.concatenate(tos, axis=0), fro).astype(BF16)
-        got = dot_nt(jnp.concatenate(picks + [counts], axis=0), ref[...])
-        total = SLOTS * len(picks)
-        out, at_row, at_sum = [], 0, total
-        for _, _, count in wants:
-            out.append((got[at_row:at_row + SLOTS * count, :], got[at_sum:at_sum + 4 * count, :]))
-            at_row, at_sum = at_row + SLOTS * count, at_sum + 4 * count
-        return out
+        return jnp.concatenate(picks + [dot_nt(jnp.concatenate(tos, axis=0), fro).astype(BF16)], axis=0)
+
+    def select(ref, idref):
+        got = dot_nt(selector(idref, [(z, 0, PLANE)]), ref[...])
+        msum[:, 0:WIDTH] += got[256:288, :]
+        return got[0:256, :]
 
     def spread(sums):
         count = sums.shape[0] // 4
@@ -197,30 +201,36 @@
 
     def pick(step, way):
         slot = at(way, step)
-        (got, sums), = select(ring.at[slot], ringi.at[slot], [(z, 0, PLANE)])
-        msum[:, 0:WIDTH] += sums
-        put(step, way, got)
-
-    def pick_beyond(way):
-        slot, wants = at(way, reach), beyond(way)
-        got = select(ring.at[slot], ringi.at[slot], [want[1:] for want in wants] + [(z, 0, PLANE)])
-        for (kind, plane, first, count), (rows, sums) in zip(wants, got):
+        put(step, way, select(ring.at[slot], ringi.at[slot]))
+
+    def last_rows(way, columns):
+        wants = beyond(way)
+        got = dot_nt(farsel[way], ring[at(way, reach), columns, :])
+        counts = [want[3] for want in wants] + [PLANE]
+        at_row, at_sum, found = 0, SLOTS * sum(counts), []
+        for count in counts:
+            found.append((got[at_row:at_row + SLOTS * count, :], got[at_sum:at_sum + 4 * count, :]))
+            at_row, at_sum = at_row + SLOTS * count, at_sum + 4 * count
+        return wants, found[:-1], found[-1]
+
+    def send_late(wants, found, part):
+        for (kind, plane, first, count), (rows, sums) in zip(wants, found):
             rows = rows + spread(sums)
-            lsend[kind, first:first + count, 0:32, :] = rows[:, 0:128].astype(BF16).reshape(count, SLOTS, 128)
-            tail = widen(rows[:, 128:]).reshape(count, 2, 16, 128)
-            tail = tail[:, 0].reshape(16 * count, 128) + pltpu.roll(tail[:, 1].reshape(16 * count, 128), 64, 1)
-            lsend[kind, first:first + count, 32:48, :] = tail.astype(BF16).reshape(count, 16, 128)
+            if part == 0:
+                lsend[kind, first:first + count, 0:32, :] = rows.astype(BF16).reshape(count, SLOTS, 128)
+            else:
+                tail = widen(rows).reshape(count, 2, 16, 128)
+                tail = tail[:, 0].reshape(16 * count, 128) + pltpu.roll(tail[:, 1].reshape(16 * count, 128), 64, 1)
+                lsend[kind, first:first + count, 32:48, :] = tail.astype(BF16).reshape(count, 16, 128)
             for o in range(count):
-                lcopy(kind, plane, first + (me + o) % count).start()
-        msum[:, 0:WIDTH] += got[-1][1]
-        return got[-1][0]
-
-    def send(step, rows):
+                lcopy(kind, plane, first + (me + o) % count, part).start()
+
+    def send(step, first=0, rows=96, sem=None):
         for o in (4, 5, 3, 2, 6, 1, 7):
-            ycopy(step, o, rows).start()
-        yrecv[step, me, 0:rows, :] = ysend[step, me, 0:rows, :]
-
-    def place(zz, rows, way, sums=False):
+            ycopy(step, o, first, rows, step if sem is None else sem).start()
+        yrecv[step, me, first:first + rows, :] = ysend[step, me, first:first + rows, :]
+
+    def placement(zz, sums=False):
         to = tgt[pl.ds(zz, 1), :]
         lane = iota((1, 256), 1) % SLOTS
         if sums:
@@ -230,24 +240,22 @@
         slot = pos % SLOTS
         hub = jnp.where((slot >= 24) & (slot < 28), zz * 32 + (pos // SLOTS) * 4 + slot - 24, -1)
         where = dot_nt(hub_hot[...], hot(hub == hub_s[...]))
-        where = (where + jnp.where(iota((512, 256), 0).astype(F32) == to, 1.0, 0.0)).astype(BF16)
+        return (where + jnp.where(iota((512, 256), 0).astype(F32) == to, 1.0, 0.0)).astype(BF16)
+
+    def place(step, way):
+        rows = jnp.concatenate([yrecv[step, :, 64 * way:64 * way + 32, :].reshape(256, 128),
+                                yrecv[step, :, 32:64, :].reshape(256, 128)], axis=1)
         acc = accp if way == 0 else accm
-        acc[...] += dot(where, rows)
-
-    def place_near(step, way, sums=False):
-        place(at(way, step), jnp.concatenate([yrecv[step, :, 64 * way:64 * way + 32, :].reshape(256, 128),
-                                              yrecv[step, :, 32:64, :].reshape(256, 128)], axis=1), way, sums)
-
-    def place_late(kind):
-        tail = lrecv[kind, :, 32:48, :].astype(F32).reshape(128, 128)
-        tail = jnp.concatenate([tail.reshape(PLANE, 1, 16, 128), pltpu.roll(tail, 64, 1).reshape(PLANE, 1, 16, 128)], axis=1)
-        rows = jnp.concatenate([lrecv[kind, :, 0:32, :].reshape(256, 128), tail.astype(BF16).reshape(256, 128)], axis=1)
-        place(at(kinds[kind][1], kinds[kind][0]), rows, 0, True)
-
-    def product(i):
-        fold = xm[i, 512:768, :]
-        carry[0:256, :] += dot(jnp.concatenate([xm[i, 0:256, :], fold], axis=1), wfold[i, 0])
-        carry[256:512, :] += dot(jnp.concatenate([xm[i, 256:512, :], fold], axis=1), wfold[i, 1])
+        acc[...] += dot(placement(at(way, step)), rows)
+
+    def product(i, part):
+        w = pl.multiple_of(i * WIDTH, 64)
+        if part == 0:
+            carry[...] += dot(xm[i, 0:512, :], wn[pl.ds(w, 128), :])
+        else:
+            b, zero = wn[pl.ds(w + 128, 64), :], jnp.zeros((64, 256), BF16)
+            carry[0:256, :] += dot(xm[i, 512:768, :], jnp.concatenate([b, zero], axis=0))
+            carry[256:512, :] += dot(xm[i, 512:768, :], jnp.concatenate([zero, b], axis=0))
 
     for load in loads[:4]:
         load.wait()
@@ -277,10 +285,8 @@
     msum[...] = jnp.zeros_like(msum)
 
     ysend[0, :, 64:96, :] = jnp.zeros((PLANE, SLOTS, 128), BF16)
-    (got, sums), = select(ft, own, [(z, 0, PLANE)])
-    msum[:, 0:WIDTH] += sums
-    put(0, 0, got)
-    send(0, 96)
+    put(0, 0, select(ft, own))
+    send(0)
 
     raw[0:24, :] = ct[...].astype(F32)
     raw[24:48, :] = jnp.full((24, 128), -1.0, F32)
@@ -295,6 +301,11 @@
         tgt[:, 128 * part:128 * part + 128] = whole
     hub_hot[...] = hot(iota((512, 512), 0) == hub_t[...])
 
+    places[:, 0:256] = placement(at(0, reach), True)
+    places[:, 256:512] = placement(at(1, reach))
+    for kind, (d, way) in enumerate(kinds):
+        places[:, 512 + 256 * kind:768 + 256 * kind] = placement(at(way, d), True)
+
     for t in range(12):
         is_at = [[(tidx[i:i + 1, t:t + 1] == b).astype(F32) for b in range(4)] for i in (0, 1)]
         block = sum(ft[:, 128 * b:128 * b + 128].astype(F32) * is_at[1][b] for b in range(4)).astype(BF16)
@@ -304,10 +315,9 @@
 
     forward(1, order)
 
-    for i in range(feats):
-        a, b, zero = wn[192 * i:192 * i + 128, :], wn[192 * i + 128:192 * i + 192, :], jnp.zeros((64, 256), BF16)
-        wfold[i, 0] = jnp.concatenate([a, b, zero], axis=0)
-        wfold[i, 1] = jnp.concatenate([a, zero, b], axis=0)
+    deg_row = deg[...].astype(F32)
+    for i in range(4):
+        degree[128 * i:128 * i + 128, :] = column(deg_row[i:i + 1, :])
 
     def own_columns():
         xf[x] = ft[...]
@@ -327,12 +337,12 @@
         forward(k, order[2:4])
         pick(k - 1, 1)
         forward(k, order[4:5])
-        send(k - 1, 96)
+        send(k - 1)
         forward(k, order[5:6])
-        yarrived(k - 2, 96)
-        place_near(k - 2, 0)
+        yarrived(k - 2)
+        place(k - 2, 0)
         forward(k, order[6:7])
-        place_near(k - 2, 1)
+        place(k - 2, 1)
 
         @pl.when(k == half // 2)
         def _():
@@ -346,63 +356,100 @@
     k = reach
     pick(k - 1, 0)
     pick(k - 1, 1)
-    send(k - 1, 96)
-    yarrived(k - 2, 96)
-    place_near(k - 2, 0)
-    place_near(k - 2, 1)
-    for piece in order:
-        zarrived(0, k, piece)
-    up_rows = pick_beyond(0)
-    for piece in order:
-        zarrived(1, k, piece)
-    down_rows = pick_beyond(1)
-    put(k, 0, up_rows + spread(msum[:, 0:WIDTH]))
-    put(k, 1, down_rows)
-    send(k, 96)
-    yarrived(k - 1, 96)
-    place_near(k - 1, 0)
-    place_near(k - 1, 1)
-    yarrived(k, 96)
-    place_near(k, 0, True)
-    place_near(k, 1)
+    send(k - 1)
+    for way in (0, 1):
+        zarrived(way, k, PIECES)
+        farsel[way] = selector(ringi.at[at(way, k)], [want[1:] for want in beyond(way)] + [(z, 0, PLANE)])
+    yarrived(k - 2)
+    place(k - 2, 0)
+    place(k - 2, 1)
+    lead, rest, split = slice(0, 128), slice(128, WIDTH), 128 // PIECE
+    near = []
+    for way in (0, 1):
+        for piece in range(split):
+            zarrived(way, k, piece)
+        wants, found, own_plane = last_rows(way, lead)
+        send_late(wants, found, 0)
+        near.append(own_plane)
+    sums = msum[:, lead] + near[0][1] + near[1][1]
+    ysend[k, :, 0:32, :] = (near[0][0] + spread(sums)).astype(BF16).reshape(PLANE, SLOTS, 128)
+    ysend[k, :, 32:64, :] = near[1][0].astype(BF16).reshape(PLANE, SLOTS, 128)
+    send(k, 0, 64)
+    near = []
+    for way in (0, 1):
+        for piece in range(split, PIECES):
+            zarrived(way, k, piece)
+        wants, found, own_plane = last_rows(way, rest)
+        send_late(wants, found, 1)
+        near.append(own_plane)
+    sums = msum[:, rest] + near[0][1] + near[1][1]
+    tail = widen(near[0][0] + spread(sums)) + pltpu.roll(widen(near[1][0]), 64, 1)
+    ysend[k, :, 64:96, :] = tail.astype(BF16).reshape(PLANE, SLOTS, 128)
+    send(k, 64, 32, k + 1)
+    yarrived(k - 1)
+    place(k - 1, 0)
+    place(k - 1, 1)
+
+    before = accp[:, lead] + accm[:, lead] + accl[:, lead]
+    yarrived(k, 0, 64)
+    larrived(0)
+    rows = jnp.concatenate([yrecv[k, :, 0:32, :].reshape(256, 128), yrecv[k, :, 32:64, :].reshape(256, 128)]
+                           + [lrecv[kind, :, 0:32, :].reshape(256, 128) for kind in range(len(kinds))], axis=0)
+    xm[x, 0:512, :] = ((before + dot(places[...], rows)) / degree[...]).astype(BF16)
+    sent = []
+
+    def tell(first):
+        for part, o in ((0, 1), (1, -1), (1, 1), (0, -1)) if feats == 4 else [(p, o) for o in range(1, feats) for p in (0, 1)]:
+            sent.append(mcopy(x, first + part, o, len(sent)))
+            sent[-1].start()
+
+    def relay(o, part):
+        marrived(-o, part)
+        sent.append(mcopy((x - o + feats) % feats, part, o, len(sent)))
+        sent[-1].start()
+
+    tell(0)
+    product(x, 0)
+
+    before = accp[:, 128:256] + pltpu.roll(accm[:, 128:256], 64, 1) + accl[:, 128:256]
+    yarrived(k, 64, 32, k + 1)
+    larrived(1)
+    both = yrecv[k, :, 64:96, :].reshape(256, 128)
+    rows = [both, pltpu.roll(both.astype(F32), 64, 1).astype(BF16)]
     for kind in range(len(kinds)):
-        larrived(kind)
-        place_late(kind)
-
-    degree = deg[...].astype(F32)
-    degree = jnp.concatenate([column(degree[i:i + 1, :]) for i in range(4)], axis=0)
-    lead = (accp[:, 0:128] + accm[:, 0:128] + accl[:, 0:128]) / degree
-    rest = (accp[:, 128:256] + pltpu.roll(accm[:, 128:256], 64, 1) + accl[:, 128:256]) / degree
-    xm[x, 0:512, :] = lead.astype(BF16)
-    xm[x, 512:768, :] = jnp.where(low, rest[0:256, :], pltpu.roll(rest[256:512, :], 64, 1)).astype(BF16)
-    sent = []
+        tail = lrecv[kind, :, 32:48, :].astype(F32).reshape(128, 128)
+        tail = jnp.concatenate([tail.reshape(PLANE, 1, 16, 128), pltpu.roll(tail, 64, 1).reshape(PLANE, 1, 16, 128)], axis=1)
+        rows.append(tail.astype(BF16).reshape(256, 128))
+    mean = (before + dot(places[...], jnp.concatenate(rows, axis=0))) / degree[...]
+    xm[x, 512:768, :] = jnp.where(low, mean[0:256, :], pltpu.roll(mean[256:512, :], 64, 1)).astype(BF16)
+    tell(2)
     if feats == 4:
-        sent = [mcopy(x, 0, 1, 0), mcopy(x, 1, -1, 1), mcopy(x, 1, 1, 2), mcopy(x, 0, -1, 3)]
-        for copy in sent:
-            copy.start()
-        product(x)
-        marrived(-1, 0)
-        sent.append(mcopy((x + 3) % 4, 0, 1, 4))
-        sent[4].start()
-        marrived(1, 1)
-        sent.append(mcopy((x + 1) % 4, 1, -1, 5))
-        sent[5].start()
+        relay(1, 0)
+        relay(-1, 1)
+        relay(1, 2)
+        relay(-1, 3)
+        product(x, 1)
         marrived(-1, 1)
-        product((x + 3) % 4)
+        product((x + 3) % 4, 0)
         marrived(1, 0)
-        product((x + 1) % 4)
+        product((x + 1) % 4, 0)
+        marrived(-1, 3)
+        product((x + 3) % 4, 1)
+        marrived(1, 2)
+        product((x + 1) % 4, 1)
         marrived(2, 0)
         marrived(2, 1)
-        product((x + 2) % 4)
+        product((x + 2) % 4, 0)
+        marrived(2, 2)
+        marrived(2, 3)
+        product((x + 2) % 4, 1)
     else:
-        sent = [mcopy(x, part, o, 2 * o + part - 2) for o in range(1, feats) for part in (0, 1)]
-        for copy in sent:
-            copy.start()
-        product(x)
+        product(x, 1)
         for o in range(1, feats):
-            marrived(o, 0)
-            marrived(o, 1)
-            product((x + o) % feats)
+            for part in range(4):
+                marrived(o, part)
+            product((x + o) % feats, 0)
+            product((x + o) % feats, 1)
     out[...] = jnp.maximum(carry[...], 0.0).astype(BF16)
 
     for way in (0, 1):
@@ -411,10 +458,13 @@
                 zcopy(way, s, piece).wait_send()
         for kind, plane, first, count in beyond(way):
             for dest in range(first, first + count):
-                lcopy(kind, plane, dest).wait_send()
+                lcopy(kind, plane, dest, 0).wait_send()
+                lcopy(kind, plane, dest, 1).wait_send()
     for o in range(1, PLANE):
-        for s in range(reach + 1):
-            ycopy(s, o, 96).wait_send()
+        for s in range(reach):
+            ycopy(s, o, 0, 96, s).wait_send()
+        ycopy(reach, o, 0, 64, reach).wait_send()
+        ycopy(reach, o, 64, 32, reach + 1).wait_send()
     for o in range(1, feats):
         fcopy(o).wait_send()
     for copy in sent:
@@ -451,7 +501,9 @@
             pltpu.VMEM((512, 256), F32),
             pltpu.VMEM((32, 256), F32),
             pltpu.VMEM((512, 512), BF16),
-            pltpu.VMEM((feats, 2, 256, 256), BF16),
+            pltpu.VMEM((2, 36 * (8 * DIRECT + 4), 512), BF16),
+            pltpu.VMEM((512, 256 * (2 * DIRECT + 1)), BF16),
+            pltpu.VMEM((512, 128), F32),
             pltpu.VMEM((512, 256), F32),
             pltpu.VMEM((IDS, 128), BF16),
             pltpu.VMEM((rings, 256), F32),
@@ -459,14 +511,14 @@
         ] + [pltpu.VMEM(a.shape, a.dtype) for a in args] + [
             pltpu.SemaphoreType.DMA((2, reach, PIECES + 1)),
             pltpu.SemaphoreType.DMA((rings, PIECES + 1)),
-            pltpu.SemaphoreType.DMA((reach + 1, PLANE)),
-            pltpu.SemaphoreType.DMA((reach + 1, PLANE)),
-            pltpu.SemaphoreType.DMA((2 * DIRECT - 1, PLANE)),
-            pltpu.SemaphoreType.DMA((2 * DIRECT - 1, PLANE)),
+            pltpu.SemaphoreType.DMA((reach + 2, PLANE)),
+            pltpu.SemaphoreType.DMA((reach + 2, PLANE)),
+            pltpu.SemaphoreType.DMA((2 * DIRECT - 1, PLANE, 2)),
+            pltpu.SemaphoreType.DMA((2 * DIRECT - 1, PLANE, 2)),
             pltpu.SemaphoreType.DMA((4,)),
             pltpu.SemaphoreType.DMA((4,)),
-            pltpu.SemaphoreType.DMA((6,)),
-            pltpu.SemaphoreType.DMA((4, 2)),
+            pltpu.SemaphoreType.DMA((12,)),
+            pltpu.SemaphoreType.DMA((4, 4)),
             pltpu.SemaphoreType.DMA((len(args),)),
         ],
         compiler_params=pltpu.CompilerParams(

time: 70.7 us -> 69.5 us (0.983)
  Pallas kernels: 68.7 us -> 67.6 us
    pallas_call x1, Pallas kernels: 68.7 us -> 67.6 us  [on_device(): pl.pallas_call(functools.partial(kernel, rings, feats), out_shape=jax.Sha...]
where the time goes in v5:
time: 69.5 us; the launch traced here: 69.2 us
  Pallas kernels  67.6 us (97%)
  local copies, waits for them, and re-layouts  1.67 us (2%)
    pallas_call x1, Pallas kernels, on_device(): pl.pallas_call(functools.partial(kernel, rings, feats), out_shape=jax.Sha...  67.6 us
    unnamed x1, local copies, waits for them, and re-layouts  1.67 us

profile of v5, /device:TPU:6, one launch (start us, length us, event | category | flops | bytes accessed | tf_op | source)
XLA Modules:
  0.0 69.2 jit_solution(2263123537618904837)
XLA Ops:
  0.0 67.6 %shard_map.136 = bf16[512,256]{1,0:T(8,128)(2,1)} custom-call(bf16[192,512]{1,0:T(8,128)(2,1)} %bitcast.16, s32[24,128]{1,0:T(8,128)} %bitcast.17, s32[24,128]{1,0:T(8,128)} %bitcast.18, s32[2,12]{1,0:T(2,128)} %bitcast.22, s32[1,4]{1,0:T(1,128)} %hl_hbm.1, s32[1,512]{1,0:T(1,128)} %ht_hbm.1, s32[1,512]{1,0:T(1,128)} %hs_hbm.1, s32[4,128]{1,0:T(4,128)} %bitcast.19, ...), custom_call_target="tpu_custom_call" | custom-call | flops 10000000000 | bytes 4000000 | tf_op jit(solution)/shard_map/pallas_call | solution.py:485
  67.6 1.7 %copy.16 = bf16[512,256]{1,0:T(8,128)(2,1)} copy(bf16[512,256]{1,0:T(8,128)(2,1)} %shard_map.136) | data formatting | bytes 524288

commit v6 on v5

--- a/solution.py
+++ b/solution.py
@@ -84,17 +84,24 @@
             src = ft_hbm.at[rows] if isinstance(step, int) and step == 0 else ring.at[slot, rows]
             dst = ring.at[slot, rows]
         return pltpu.make_async_remote_copy(
-            src_ref=src, dst_ref=dst, send_sem=zs.at[way, step, piece], recv_sem=zr.at[slot, piece],
+            src_ref=src, dst_ref=dst, send_sem=zs.at[way, step, piece // PIECES], recv_sem=zr.at[slot, piece],
             device_id=(up if way == 0 else down, x), device_id_type=MESH)
 
     def zarrived(way, step, piece):
         slot = at(way, step)
         ref = ringi.at[slot] if piece == PIECES else ring.at[slot, pl.ds(piece * PIECE, PIECE)]
         pltpu.make_async_remote_copy(
-            src_ref=ref, dst_ref=ref, send_sem=zs.at[way, 0, piece], recv_sem=zr.at[slot, piece],
+            src_ref=ref, dst_ref=ref, send_sem=zs.at[way, 0, piece // PIECES], recv_sem=zr.at[slot, piece],
             device_id=(up, x), device_id_type=MESH).wait_recv()
 
     order = (PIECES,) + tuple(range(PIECES))
+
+    def zsent(way, step):
+        slot = at(way, step)
+        for ref, sem in ((ring.at[slot], 0), (ringi.at[slot], 1)):
+            pltpu.make_async_remote_copy(
+                src_ref=ref, dst_ref=ref, send_sem=zs.at[way, step, sem], recv_sem=zr.at[slot, 0],
+                device_id=(up, x), device_id_type=MESH).wait_send()
 
     def forward(step, pieces):
         for piece in pieces:
@@ -131,16 +138,13 @@
     def lcopy(kind, plane, dest, part):
         return pltpu.make_async_remote_copy(
             src_ref=lsend.at[kind, dest, late[part]], dst_ref=lrecv.at[kind, me, late[part]],
-            send_sem=ls.at[kind, dest, part], recv_sem=lr.at[kind, me, part],
+            send_sem=ls.at[part], recv_sem=lr.at[part],
             device_id=(plane * PLANE + dest, x), device_id_type=MESH)
 
-    def larrived(part):
-        for kind in range(len(kinds)):
-            for src in range(PLANE):
-                ref = lrecv.at[kind, src, late[part]]
-                pltpu.make_async_remote_copy(
-                    src_ref=ref, dst_ref=ref, send_sem=ls.at[kind, src, part], recv_sem=lr.at[kind, src, part],
-                    device_id=(up, x), device_id_type=MESH).wait_recv()
+    def lall(part):
+        return pltpu.make_async_remote_copy(
+            src_ref=lsend.at[:, :, late[part]], dst_ref=lrecv.at[:, :, late[part]], send_sem=ls.at[part], recv_sem=lr.at[part],
+            device_id=(up, x), device_id_type=MESH)
 
     def fcopy(o):
         return pltpu.make_async_remote_copy(
@@ -390,9 +394,17 @@
     place(k - 1, 0)
     place(k - 1, 1)
 
+    for s in range(reach):
+        for way in (0, 1):
+            zsent(way, s)
+        for o in range(1, PLANE):
+            ycopy(s, o, 0, 96, s).wait_send()
+    for o in range(1, feats):
+        fcopy(o).wait_send()
+
     before = accp[:, lead] + accm[:, lead] + accl[:, lead]
     yarrived(k, 0, 64)
-    larrived(0)
+    lall(0).wait_recv()
     rows = jnp.concatenate([yrecv[k, :, 0:32, :].reshape(256, 128), yrecv[k, :, 32:64, :].reshape(256, 128)]
                            + [lrecv[kind, :, 0:32, :].reshape(256, 128) for kind in range(len(kinds))], axis=0)
     xm[x, 0:512, :] = ((before + dot(places[...], rows)) / degree[...]).astype(BF16)
@@ -408,12 +420,19 @@
         sent.append(mcopy((x - o + feats) % feats, part, o, len(sent)))
         sent[-1].start()
 
+    def done():
+        lall(0).wait_send()
+        lall(1).wait_send()
+        for o in range(1, PLANE):
+            ycopy(k, o, 0, 64, k).wait_send()
+            ycopy(k, o, 64, 32, k + 1).wait_send()
+
     tell(0)
     product(x, 0)
 
     before = accp[:, 128:256] + pltpu.roll(accm[:, 128:256], 64, 1) + accl[:, 128:256]
     yarrived(k, 64, 32, k + 1)
-    larrived(1)
+    lall(1).wait_recv()
     both = yrecv[k, :, 64:96, :].reshape(256, 128)
     rows = [both, pltpu.roll(both.astype(F32), 64, 1).astype(BF16)]
     for kind in range(len(kinds)):
@@ -429,6 +448,7 @@
         relay(1, 2)
         relay(-1, 3)
         product(x, 1)
+        done()
         marrived(-1, 1)
         product((x + 3) % 4, 0)
         marrived(1, 0)
@@ -445,6 +465,7 @@
         product((x + 2) % 4, 1)
     else:
         product(x, 1)
+        done()
         for o in range(1, feats):
             for part in range(4):
                 marrived(o, part)
@@ -452,21 +473,6 @@
             product((x + o) % feats, 1)
     out[...] = jnp.maximum(carry[...], 0.0).astype(BF16)
 
-    for way in (0, 1):
-        for s in range(reach):
-            for piece in order:
-                zcopy(way, s, piece).wait_send()
-        for kind, plane, first, count in beyond(way):
-            for dest in range(first, first + count):
-                lcopy(kind, plane, dest, 0).wait_send()
-                lcopy(kind, plane, dest, 1).wait_send()
-    for o in range(1, PLANE):
-        for s in range(reach):
-            ycopy(s, o, 0, 96, s).wait_send()
-        ycopy(reach, o, 0, 64, reach).wait_send()
-        ycopy(reach, o, 64, 32, reach + 1).wait_send()
-    for o in range(1, feats):
-        fcopy(o).wait_send()
     for copy in sent:
         copy.wait_send()
 
@@ -484,7 +490,7 @@
         args = args[:1] + tuple(jnp.pad(a, ((0, 0), (0, 128 - parts))) for a in args[1:3]) + args[3:]
     return pl.pallas_call(
         functools.partial(kernel, rings, feats),
-        out_shape=jax.ShapeDtypeStruct((512, 256), BF16),
+        out_shape=pltpu.VMEM((512, 256), BF16),
         in_specs=[anywhere] * len(args),
         out_specs=pl.BlockSpec(memory_space=pltpu.VMEM),
         scratch_shapes=[
@@ -509,12 +515,12 @@
             pltpu.VMEM((rings, 256), F32),
             pltpu.VMEM((IDS, 128), F32),
         ] + [pltpu.VMEM(a.shape, a.dtype) for a in args] + [
-            pltpu.SemaphoreType.DMA((2, reach, PIECES + 1)),
+            pltpu.SemaphoreType.DMA((2, reach, 2)),
             pltpu.SemaphoreType.DMA((rings, PIECES + 1)),
             pltpu.SemaphoreType.DMA((reach + 2, PLANE)),
             pltpu.SemaphoreType.DMA((reach + 2, PLANE)),
-            pltpu.SemaphoreType.DMA((2 * DIRECT - 1, PLANE, 2)),
-            pltpu.SemaphoreType.DMA((2 * DIRECT - 1, PLANE, 2)),
+            pltpu.SemaphoreType.DMA((2,)),
+            pltpu.SemaphoreType.DMA((2,)),
             pltpu.SemaphoreType.DMA((4,)),
             pltpu.SemaphoreType.DMA((4,)),
             pltpu.SemaphoreType.DMA((12,)),

time: 69.5 us -> 66.1 us (0.951)
  Pallas kernels: 67.6 us -> 65.2 us
  local copies, waits for them, and re-layouts: 1.67 us -> 0.71 us
    pallas_call x1, Pallas kernels: 67.6 us -> 65.2 us  [on_device(): pl.pallas_call(functools.partial(kernel, rings, feats), out_shape=pltpu.V...]
    unnamed x1, local copies, waits for them, and re-layouts: 1.67 us -> 0.71 us
where the time goes in v6:
time: 66.1 us; the launch traced here: 65.9 us
  Pallas kernels  65.2 us (99%)
  local copies, waits for them, and re-layouts  0.71 us (1%)
    pallas_call x1, Pallas kernels, on_device(): pl.pallas_call(functools.partial(kernel, rings, feats), out_shape=pltpu.V...  65.2 us

profile of v6, /device:TPU:6, one launch (start us, length us, event | category | flops | bytes accessed | tf_op | source)
XLA Modules:
  0.0 65.9 jit_solution(17765183569382386972)
XLA Ops:
  0.0 65.2 %shard_map.136 = bf16[512,256]{1,0:T(8,128)(2,1)S(1)} custom-call(bf16[192,512]{1,0:T(8,128)(2,1)} %bitcast.16, s32[24,128]{1,0:T(8,128)} %bitcast.17, s32[24,128]{1,0:T(8,128)} %bitcast.18, s32[2,12]{1,0:T(2,128)} %bitcast.22, s32[1,4]{1,0:T(1,128)} %hl_hbm.1, s32[1,512]{1,0:T(1,128)} %ht_hbm.1, s32[1,512]{1,0:T(1,128)} %hs_hbm.1, s32[4,128]{1,0:T(4,128)} %bitcast.19, ...), custom_call_target="tpu_custom_call" | custom-call | flops 10000000000 | bytes 4000000 | tf_op jit(solution)/shard_map/pallas_call | solution.py:491
  65.2 0.7 %copy.16 = bf16[512,256]{1,0:T(8,128)(2,1)} copy(bf16[512,256]{1,0:T(8,128)(2,1)S(1)} %shard_map.136) | data formatting | bytes 524288

commit v7 on v6

--- a/solution.py
+++ b/solution.py
@@ -43,7 +43,7 @@
 
 
 def kernel(rings, feats, ft_hbm, cs_hbm, ct_hbm, ti_hbm, hl_hbm, ht_hbm, hs_hbm, mf_hbm, mt_hbm, deg_hbm, bias_hbm,
-           mask_hbm, ws_hbm, wn_hbm, out, ring, ringi, ysend, yrecv, lsend, lrecv, xf, xm, accp, accm, accl, msum, hub_hot, farsel, places, degree, carry,
+           mask_hbm, ws_hbm, wn_hbm, out, ring, ringi, ysend, yrecv, lsend, lrecv, xf, xm, accp, accm, accl, msum, hub_hot, farsel, places, degree, spot, carry,
            own, tgt, raw, ft, cs, ct, tidx, hub_local, hub_t, hub_s, mirror_f, mirror_t, deg, bias, mask, ws, wn,
            zs, zr, ys, yr, ls, lr, fs, fr, ms, mr, local):
     half = rings // 2
@@ -188,8 +188,7 @@
 
     def spread(sums):
         count = sums.shape[0] // 4
-        row, col = iota((SLOTS * count, 4 * count), 0), iota((SLOTS * count, 4 * count), 1)
-        return dot(hot((row // SLOTS == col // 4) & (row % SLOTS == 28 + col % 4)), sums.astype(BF16))
+        return dot(spot[0:SLOTS * count, 0:4 * count], sums.astype(BF16))
 
     def widen(tail):
         return jnp.concatenate([tail, jnp.zeros_like(tail)], axis=1)
@@ -304,36 +303,54 @@
             whole = jnp.where(lane // SLOTS == d, pltpu.roll(one, SLOTS * d, 1) if d else one, whole)
         tgt[:, 128 * part:128 * part + 128] = whole
     hub_hot[...] = hot(iota((512, 512), 0) == hub_t[...])
-
-    places[:, 0:256] = placement(at(0, reach), True)
-    places[:, 256:512] = placement(at(1, reach))
-    for kind, (d, way) in enumerate(kinds):
-        places[:, 512 + 256 * kind:768 + 256 * kind] = placement(at(way, d), True)
-
-    for t in range(12):
-        is_at = [[(tidx[i:i + 1, t:t + 1] == b).astype(F32) for b in range(4)] for i in (0, 1)]
-        block = sum(ft[:, 128 * b:128 * b + 128].astype(F32) * is_at[1][b] for b in range(4)).astype(BF16)
-        part = dot_nt(mask[t].astype(F32).astype(BF16), block)
-        for b in range(4):
-            accl[128 * b:128 * b + 128, 0:WIDTH] += part * is_at[0][b]
-
-    forward(1, order)
+    row, col = iota((256, 32), 0), iota((256, 32), 1)
+    spot[...] = hot((row // SLOTS == col // 4) & (row % SLOTS == 28 + col % 4))
+
+    def tiles(first, last):
+        for t in range(first, last):
+            is_at = [[(tidx[i:i + 1, t:t + 1] == b).astype(F32) for b in range(4)] for i in (0, 1)]
+            block = sum(ft[:, 128 * b:128 * b + 128].astype(F32) * is_at[1][b] for b in range(4)).astype(BF16)
+            part = dot_nt(mask[t].astype(F32).astype(BF16), block)
+            for b in range(4):
+                accl[128 * b:128 * b + 128, 0:WIDTH] += part * is_at[0][b]
+
+    def last_place(i):
+        if i < 2:
+            places[:, 256 * i:256 * i + 256] = placement(at(i, reach), i == 0)
+        else:
+            d, way = kinds[i - 2]
+            places[:, 256 * i:256 * i + 256] = placement(at(way, d), True)
+
+    tiles(0, 3)
+    forward(1, order[0:2])
+    tiles(3, 6)
+    forward(1, order[2:3])
+    tiles(6, 9)
+    forward(1, order[3:4])
+    tiles(9, 12)
+    forward(1, order[4:5])
+    last_place(0)
+    last_place(1)
+    forward(1, order[5:6])
+    last_place(2)
+    forward(1, order[6:7])
+    for i in range(3, 2 + len(kinds)):
+        last_place(i)
 
     deg_row = deg[...].astype(F32)
     for i in range(4):
         degree[128 * i:128 * i + 128, :] = column(deg_row[i:i + 1, :])
 
-    def own_columns():
-        xf[x] = ft[...]
-        for o in range(1, feats):
+    def own_columns(o):
+        i = (x + o) % feats
+        if isinstance(o, int) and o == 0:
+            xf[x] = ft[...]
+            carry[...] = jnp.zeros_like(carry) + bias[...]
+        else:
             farrived(o)
-        carry[...] = jnp.zeros_like(carry) + bias[...]
-
-        def one(i, _):
-            carry[...] += dot_tn(xf[i], ws[pl.ds(pl.multiple_of(i * WIDTH, 64), WIDTH), :])
-            return 0
-
-        lax.fori_loop(0, feats, one, 0)
+        carry[...] += dot_tn(xf[i], ws[pl.ds(pl.multiple_of(i * WIDTH, 64), WIDTH), :])
+
+    own_columns(0)
 
     def step(k, _):
         forward(k, order[:2])
@@ -343,19 +360,25 @@
         forward(k, order[4:5])
         send(k - 1)
         forward(k, order[5:6])
-        yarrived(k - 2)
-        place(k - 2, 0)
+
+        @pl.when(k >= 3)
+        def _():
+            yarrived(k - 3)
+            place(k - 3, 0)
         forward(k, order[6:7])
-        place(k - 2, 1)
-
-        @pl.when(k == half // 2)
+
+        @pl.when(k >= 3)
         def _():
-            own_columns()
+            place(k - 3, 1)
+
+        @pl.when(k - 1 < feats)
+        def _():
+            own_columns(k - 1)
         return 0
 
     lax.fori_loop(2, reach, step, 0)
-    if not 2 <= half // 2 < reach:
-        own_columns()
+    for o in range(max(1, reach - 1), feats):
+        own_columns(o)
 
     k = reach
     pick(k - 1, 0)
@@ -364,9 +387,10 @@
     for way in (0, 1):
         zarrived(way, k, PIECES)
         farsel[way] = selector(ringi.at[at(way, k)], [want[1:] for want in beyond(way)] + [(z, 0, PLANE)])
-    yarrived(k - 2)
-    place(k - 2, 0)
-    place(k - 2, 1)
+    for s in range(max(0, k - 3), k - 1):
+        yarrived(s)
+        place(s, 0)
+        place(s, 1)
     lead, rest, split = slice(0, 128), slice(128, WIDTH), 128 // PIECE
     near = []
     for way in (0, 1):
@@ -510,6 +534,7 @@
             pltpu.VMEM((2, 36 * (8 * DIRECT + 4), 512), BF16),
             pltpu.VMEM((512, 256 * (2 * DIRECT + 1)), BF16),
             pltpu.VMEM((512, 128), F32),
+            pltpu.VMEM((256, 32), BF16),
             pltpu.VMEM((512, 256), F32),
             pltpu.VMEM((IDS, 128), BF16),
             pltpu.VMEM((rings, 256), F32),

time: 66.1 us -> 65.7 us (level)
  no operation moved by 1% of the time
where the time goes in v7:
time: 65.7 us; the launch traced here: 65.5 us
  Pallas kernels  64.8 us (99%)
  local copies, waits for them, and re-layouts  0.71 us (1%)
    pallas_call x1, Pallas kernels, on_device(): pl.pallas_call(functools.partial(kernel, rings, feats), out_shape=pltpu.V...  64.8 us

profile of v7, /device:TPU:6, one launch (start us, length us, event | category | flops | bytes accessed | tf_op | source)
XLA Modules:
  0.0 65.5 jit_solution(12387348990663012194)
XLA Ops:
  0.0 64.8 %shard_map.136 = bf16[512,256]{1,0:T(8,128)(2,1)S(1)} custom-call(bf16[192,512]{1,0:T(8,128)(2,1)} %bitcast.16, s32[24,128]{1,0:T(8,128)} %bitcast.17, s32[24,128]{1,0:T(8,128)} %bitcast.18, s32[2,12]{1,0:T(2,128)} %bitcast.22, s32[1,4]{1,0:T(1,128)} %hl_hbm.1, s32[1,512]{1,0:T(1,128)} %ht_hbm.1, s32[1,512]{1,0:T(1,128)} %hs_hbm.1, s32[4,128]{1,0:T(4,128)} %bitcast.19, ...), custom_call_target="tpu_custom_call" | custom-call | flops 10000000000 | bytes 4000000 | tf_op jit(solution)/shard_map/pallas_call | solution.py:515
  64.8 0.7 %copy.16 = bf16[512,256]{1,0:T(8,128)(2,1)} copy(bf16[512,256]{1,0:T(8,128)(2,1)S(1)} %shard_map.136) | data formatting | bytes 524288

commit v8 on v7

--- a/solution.py
+++ b/solution.py
@@ -84,23 +84,23 @@
             src = ft_hbm.at[rows] if isinstance(step, int) and step == 0 else ring.at[slot, rows]
             dst = ring.at[slot, rows]
         return pltpu.make_async_remote_copy(
-            src_ref=src, dst_ref=dst, send_sem=zs.at[way, step, piece // PIECES], recv_sem=zr.at[slot, piece],
+            src_ref=src, dst_ref=dst, send_sem=zs.at[piece // PIECES], recv_sem=zr.at[slot, piece],
             device_id=(up if way == 0 else down, x), device_id_type=MESH)
 
     def zarrived(way, step, piece):
         slot = at(way, step)
         ref = ringi.at[slot] if piece == PIECES else ring.at[slot, pl.ds(piece * PIECE, PIECE)]
         pltpu.make_async_remote_copy(
-            src_ref=ref, dst_ref=ref, send_sem=zs.at[way, 0, piece // PIECES], recv_sem=zr.at[slot, piece],
+            src_ref=ref, dst_ref=ref, send_sem=zs.at[0], recv_sem=zr.at[slot, piece],
             device_id=(up, x), device_id_type=MESH).wait_recv()
 
     order = (PIECES,) + tuple(range(PIECES))
 
-    def zsent(way, step):
-        slot = at(way, step)
-        for ref, sem in ((ring.at[slot], 0), (ringi.at[slot], 1)):
+    def zsent():
+        for buf, sem in ((ring, 0), (ringi, 1)):
+            ref = buf.at[pl.ds(0, 2 * reach)]
             pltpu.make_async_remote_copy(
-                src_ref=ref, dst_ref=ref, send_sem=zs.at[way, step, sem], recv_sem=zr.at[slot, 0],
+                src_ref=ref, dst_ref=ref, send_sem=zs.at[sem], recv_sem=zr.at[0, 0],
                 device_id=(up, x), device_id_type=MESH).wait_send()
 
     def forward(step, pieces):
@@ -113,16 +113,18 @@
         dest = (me + o) % PLANE
         return pltpu.make_async_remote_copy(
             src_ref=ysend.at[step, dest, pl.ds(first, rows)], dst_ref=yrecv.at[step, me, pl.ds(first, rows)],
-            send_sem=ys.at[sem, o - 1], recv_sem=yr.at[sem, me],
+            send_sem=ys.at[sem], recv_sem=yr.at[sem],
             device_id=(z * PLANE + dest, x), device_id_type=MESH)
 
+    def yall(step, first=0, rows=96, sem=None):
+        sem = step if sem is None else sem
+        return pltpu.make_async_remote_copy(
+            src_ref=ysend.at[step, pl.ds(0, PLANE - 1), pl.ds(first, rows)],
+            dst_ref=yrecv.at[step, pl.ds(0, PLANE - 1), pl.ds(first, rows)],
+            send_sem=ys.at[sem], recv_sem=yr.at[sem], device_id=(up, x), device_id_type=MESH)
+
     def yarrived(step, first=0, rows=96, sem=None):
-        for o in range(1, PLANE):
-            src = (me + o) % PLANE
-            ref = yrecv.at[step, src, pl.ds(first, rows)]
-            pltpu.make_async_remote_copy(
-                src_ref=ref, dst_ref=ref, send_sem=ys.at[step, o - 1], recv_sem=yr.at[step if sem is None else sem, src],
-                device_id=(z * PLANE + src, x), device_id_type=MESH).wait_recv()
+        yall(step, first, rows, sem).wait_recv()
 
     kinds = [(d, way) for d in range(reach + 1, half) for way in (0, 1)] + [(half, 0)]
 
@@ -317,9 +319,11 @@
     def last_place(i):
         if i < 2:
             places[:, 256 * i:256 * i + 256] = placement(at(i, reach), i == 0)
-        else:
+        elif i < 2 + len(kinds):
             d, way = kinds[i - 2]
             places[:, 256 * i:256 * i + 256] = placement(at(way, d), True)
+        else:
+            places[:, 256 * i:256 * i + 256] = placement(at(i - 2 - len(kinds), reach - 1))
 
     tiles(0, 3)
     forward(1, order[0:2])
@@ -334,7 +338,7 @@
     forward(1, order[5:6])
     last_place(2)
     forward(1, order[6:7])
-    for i in range(3, 2 + len(kinds)):
+    for i in range(3, 4 + len(kinds)):
         last_place(i)
 
     deg_row = deg[...].astype(F32)
@@ -415,14 +419,9 @@
     ysend[k, :, 64:96, :] = tail.astype(BF16).reshape(PLANE, SLOTS, 128)
     send(k, 64, 32, k + 1)
     yarrived(k - 1)
-    place(k - 1, 0)
-    place(k - 1, 1)
-
+    zsent()
     for s in range(reach):
-        for way in (0, 1):
-            zsent(way, s)
-        for o in range(1, PLANE):
-            ycopy(s, o, 0, 96, s).wait_send()
+        yall(s).wait_send()
     for o in range(1, feats):
         fcopy(o).wait_send()
 
@@ -430,7 +429,8 @@
     yarrived(k, 0, 64)
     lall(0).wait_recv()
     rows = jnp.concatenate([yrecv[k, :, 0:32, :].reshape(256, 128), yrecv[k, :, 32:64, :].reshape(256, 128)]
-                           + [lrecv[kind, :, 0:32, :].reshape(256, 128) for kind in range(len(kinds))], axis=0)
+                           + [lrecv[kind, :, 0:32, :].reshape(256, 128) for kind in range(len(kinds))]
+                           + [yrecv[k - 1, :, 64 * way:64 * way + 32, :].reshape(256, 128) for way in (0, 1)], axis=0)
     xm[x, 0:512, :] = ((before + dot(places[...], rows)) / degree[...]).astype(BF16)
     sent = []
 
@@ -447,9 +447,8 @@
     def done():
         lall(0).wait_send()
         lall(1).wait_send()
-        for o in range(1, PLANE):
-            ycopy(k, o, 0, 64, k).wait_send()
-            ycopy(k, o, 64, 32, k + 1).wait_send()
+        yall(k, 0, 64, k).wait_send()
+        yall(k, 64, 32, k + 1).wait_send()
 
     tell(0)
     product(x, 0)
@@ -463,6 +462,8 @@
         tail = lrecv[kind, :, 32:48, :].astype(F32).reshape(128, 128)
         tail = jnp.concatenate([tail.reshape(PLANE, 1, 16, 128), pltpu.roll(tail, 64, 1).reshape(PLANE, 1, 16, 128)], axis=1)
         rows.append(tail.astype(BF16).reshape(256, 128))
+    both = yrecv[k - 1, :, 32:64, :].reshape(256, 128)
+    rows += [both, pltpu.roll(both.astype(F32), 64, 1).astype(BF16)]
     mean = (before + dot(places[...], jnp.concatenate(rows, axis=0))) / degree[...]
     xm[x, 512:768, :] = jnp.where(low, mean[0:256, :], pltpu.roll(mean[256:512, :], 64, 1)).astype(BF16)
     tell(2)
@@ -532,7 +533,7 @@
             pltpu.VMEM((32, 256), F32),
             pltpu.VMEM((512, 512), BF16),
             pltpu.VMEM((2, 36 * (8 * DIRECT + 4), 512), BF16),
-            pltpu.VMEM((512, 256 * (2 * DIRECT + 1)), BF16),
+            pltpu.VMEM((512, 256 * (2 * DIRECT + 3)), BF16),
             pltpu.VMEM((512, 128), F32),
             pltpu.VMEM((256, 32), BF16),
             pltpu.VMEM((512, 256), F32),
@@ -540,10 +541,10 @@
             pltpu.VMEM((rings, 256), F32),
             pltpu.VMEM((IDS, 128), F32),
         ] + [pltpu.VMEM(a.shape, a.dtype) for a in args] + [
-            pltpu.SemaphoreType.DMA((2, reach, 2)),
+            pltpu.SemaphoreType.DMA((2,)),
             pltpu.SemaphoreType.DMA((rings, PIECES + 1)),
-            pltpu.SemaphoreType.DMA((reach + 2, PLANE)),
-            pltpu.SemaphoreType.DMA((reach + 2, PLANE)),
+            pltpu.SemaphoreType.DMA((reach + 2,)),
+            pltpu.SemaphoreType.DMA((reach + 2,)),
             pltpu.SemaphoreType.DMA((2,)),
             pltpu.SemaphoreType.DMA((2,)),
             pltpu.SemaphoreType.DMA((4,)),

time: 65.7 us -> 64.8 us (0.986)
  Pallas kernels: 64.8 us -> 63.8 us
    pallas_call x1, Pallas kernels: 64.8 us -> 63.8 us  [on_device(): pl.pallas_call(functools.partial(kernel, rings, feats), out_shape=pltpu.V...]
where the time goes in v8:
time: 64.8 us; the launch traced here: 64.6 us
  Pallas kernels  63.8 us (98%)
  local copies, waits for them, and re-layouts  0.71 us (1%)
    pallas_call x1, Pallas kernels, on_device(): pl.pallas_call(functools.partial(kernel, rings, feats), out_shape=pltpu.V...  63.8 us

profile of v8, /device:TPU:6, one launch (start us, length us, event | category | flops | bytes accessed | tf_op | source)
XLA Modules:
  0.0 64.6 jit_solution(7997964688324406877)
XLA Ops:
  0.0 63.8 %shard_map.136 = bf16[512,256]{1,0:T(8,128)(2,1)S(1)} custom-call(bf16[192,512]{1,0:T(8,128)(2,1)} %bitcast.16, s32[24,128]{1,0:T(8,128)} %bitcast.17, s32[24,128]{1,0:T(8,128)} %bitcast.18, s32[2,12]{1,0:T(2,128)} %bitcast.22, s32[1,4]{1,0:T(1,128)} %hl_hbm.1, s32[1,512]{1,0:T(1,128)} %ht_hbm.1, s32[1,512]{1,0:T(1,128)} %hs_hbm.1, s32[4,128]{1,0:T(4,128)} %bitcast.19, ...), custom_call_target="tpu_custom_call" | custom-call | flops 10000000000 | bytes 4000000 | tf_op jit(solution)/shard_map/pallas_call | solution.py:516
  63.9 0.7 %copy.16 = bf16[512,256]{1,0:T(8,128)(2,1)} copy(bf16[512,256]{1,0:T(8,128)(2,1)S(1)} %shard_map.136) | data formatting | bytes 524288

commit v9 on v8

--- a/solution.py
+++ b/solution.py
@@ -391,10 +391,6 @@
     for way in (0, 1):
         zarrived(way, k, PIECES)
         farsel[way] = selector(ringi.at[at(way, k)], [want[1:] for want in beyond(way)] + [(z, 0, PLANE)])
-    for s in range(max(0, k - 3), k - 1):
-        yarrived(s)
-        place(s, 0)
-        place(s, 1)
     lead, rest, split = slice(0, 128), slice(128, WIDTH), 128 // PIECE
     near = []
     for way in (0, 1):
@@ -418,6 +414,10 @@
     tail = widen(near[0][0] + spread(sums)) + pltpu.roll(widen(near[1][0]), 64, 1)
     ysend[k, :, 64:96, :] = tail.astype(BF16).reshape(PLANE, SLOTS, 128)
     send(k, 64, 32, k + 1)
+    for s in range(max(0, k - 3), k - 1):
+        yarrived(s)
+        place(s, 0)
+        place(s, 1)
     yarrived(k - 1)
     zsent()
     for s in range(reach):

time: 64.8 us -> 63 us (0.972)
  Pallas kernels: 63.8 us -> 61.4 us
    pallas_call x1, Pallas kernels: 63.8 us -> 61.4 us  [on_device(): pl.pallas_call(functools.partial(kernel, rings, feats), out_shape=pltpu.V...]
where the time goes in v9:
time: 63 us; the launch traced here: 62.2 us
  Pallas kernels  61.4 us (97%)
  local copies, waits for them, and re-layouts  0.71 us (1%)
    pallas_call x1, Pallas kernels, on_device(): pl.pallas_call(functools.partial(kernel, rings, feats), out_shape=pltpu.V...  61.4 us

profile of v9, /device:TPU:6, one launch (start us, length us, event | category | flops | bytes accessed | tf_op | source)
XLA Modules:
  0.0 62.2 jit_solution(11550909059027507349)
XLA Ops:
  0.0 61.4 %shard_map.136 = bf16[512,256]{1,0:T(8,128)(2,1)S(1)} custom-call(bf16[192,512]{1,0:T(8,128)(2,1)} %bitcast.16, s32[24,128]{1,0:T(8,128)} %bitcast.17, s32[24,128]{1,0:T(8,128)} %bitcast.18, s32[2,12]{1,0:T(2,128)} %bitcast.22, s32[1,4]{1,0:T(1,128)} %hl_hbm.1, s32[1,512]{1,0:T(1,128)} %ht_hbm.1, s32[1,512]{1,0:T(1,128)} %hs_hbm.1, s32[4,128]{1,0:T(4,128)} %bitcast.19, ...), custom_call_target="tpu_custom_call" | custom-call | flops 10000000000 | bytes 4000000 | tf_op jit(solution)/shard_map/pallas_call | solution.py:516
  61.4 0.7 %copy.16 = bf16[512,256]{1,0:T(8,128)(2,1)} copy(bf16[512,256]{1,0:T(8,128)(2,1)S(1)} %shard_map.136) | data formatting | bytes 524288
